TPU v7x, 256 devices: a whole 4x4x8 slice. The times are simulated.
256 devices in a mesh: dp: 16 (over x, y), mp: 16 (over z, core).
Axes of the slice: x: 4, y: 4, z: 8, core: 2. Of those that a mesh axis runs over, the one named last changes fastest.
Arguments:
- tokens: bfloat16 [2048, 8192], P('dp', 'mp'), may hold values from -6 to 6
- gate_tiles: bfloat16 [65536, 128], P('mp'), may hold values from -0.3125 to 0.3125
- gate_index: int32 [2048, 2], P('mp'), may hold values from 0 to 223, as said below
- gate_count: int32 [256], P('mp'), may hold values from 1 to 8, as said below
- up_tiles: bfloat16 [65536, 128], P('mp'), may hold values from -0.3125 to 0.3125
- up_index: int32 [2048, 2], P('mp'), may hold values from 0 to 223, as said below
- up_count: int32 [256], P('mp'), may hold values from 1 to 8, as said below
- down_tiles: bfloat16 [65536, 128], P('mp'), may hold values from -0.25 to 0.25
- down_index: int32 [2048, 2], P('mp'), may hold values from 0 to 223, as said below
- down_count: int32 [256], P('mp'), may hold values from 1 to 8, as said below
- grad_output: bfloat16 [2048, 8192], P('dp', 'mp'), may hold values from -6 to 6
Outputs:
- layer_output: bfloat16 [2048, 8192], P('dp', 'mp')
- grad_tokens: bfloat16 [2048, 8192], P('dp', 'mp')
- grad_gate: bfloat16 [65536, 128], P('mp')
- grad_up: bfloat16 [65536, 128], P('mp')
- grad_down: bfloat16 [65536, 128], P('mp')
Inputs may be any that keep to these rules, and one draw needn't show every extreme that they name: In each of gate_index and up_index, entry k = (q * 16 + e) * 8 + c has its row block (column 0) among q * 8 to (q + 1) * 8 - 1 and its column block (column 1) among e * 14 to (e + 1) * 14 - 1; the 128 entries of one q name distinct blocks. `up_index`: as for gate_index, drawn apart. `down_index`: entry k = (q * 16 + e) * 8 + c has its row block (column 0) among q * 14 to (q + 1) * 14 - 1 of the hidden blocks and its column block (column 1) among e * 8 to (e + 1) * 8 - 1; the 128 entries of one q name distinct blocks. `gate_count`: some e has count 8 from every q. `up_count`: some e has count 8 from every q. `down_count`: some e has count 8 from every q.
All inputs are finite; a program needn't handle non-finite values.
Results may differ from a plain program's by a relative error of at most 0.03.
Values may be sent and summed in bfloat16 or wider, within the bound.
No kernel may reach another device: no remote copies, remote signals or barrier semaphores. Data moves between devices by JAX's collectives and lax.ppermute only.
A program may use at most 128 MiB of HBM per device.

v0:
```python
import jax
import jax.numpy as jnp
from jax import lax
from jax.sharding import PartitionSpec as P

FF = 14336
TILE = 64


HIGH = lax.Precision.HIGHEST


def rounded(values):
    return values.astype(jnp.bfloat16).astype(jnp.float32)


def select_blocks(values, hot_table, shared):
    if shared:
        form = "tri,gcr->tgci"
    else:
        form = "tgri,gcr->tgci"
    picked = jnp.einsum(
        form, values, hot_table.astype(jnp.bfloat16), preferred_element_type=jnp.float32
    )
    return picked.astype(jnp.bfloat16)


def place_blocks(product, hot_table, shared):
    if shared:
        form = "tgci,gcr->tri"
    else:
        form = "tgci,gcr->tgri"
    return jnp.einsum(form, product, hot_table, precision=HIGH)


def tile_forward(left_rows, tile_values, row_table, col_table):
    picked = select_blocks(left_rows, row_table, True)
    product = jnp.einsum("tgci,gcij->tgcj", picked, tile_values, preferred_element_type=jnp.float32)
    return place_blocks(product, col_table, False)


def tile_backward(right_rows, tile_values, row_table, col_table, out_shared):
    picked = select_blocks(right_rows, col_table, False)
    product = jnp.einsum("tgcj,gcij->tgci", picked, tile_values, preferred_element_type=jnp.float32)
    return place_blocks(product, row_table, out_shared)


def tile_grads(left_rows, right_rows, row_table, col_table):
    left_picked = select_blocks(left_rows, row_table, True)
    right_picked = select_blocks(right_rows, col_table, False)
    return jnp.einsum(
        "tgci,tgcj->gcij", left_picked, right_picked, preferred_element_type=jnp.float32
    )


def block_tables(rows_local, cols_local, valid_mask, row_size, col_size):
    row_table = (rows_local[..., None] == jnp.arange(row_size, dtype=jnp.int32)).astype(
        jnp.float32
    ) * valid_mask[..., None]
    col_table = (cols_local[..., None] == jnp.arange(col_size, dtype=jnp.int32)).astype(jnp.float32)
    return (row_table, col_table)


def per_device(
    tokens,
    gate_tiles,
    gate_index,
    gate_count,
    up_tiles,
    up_index,
    up_count,
    down_tiles,
    down_index,
    down_count,
    grad_output,
):
    groups = lax.axis_size("mp")
    owner_index = lax.axis_index("mp")
    tile_size = TILE
    tok_rows = tokens.shape[0]
    d_own = tokens.shape[1] // tile_size
    f_own = FF // tile_size // groups
    slots = gate_index.shape[0]
    bucket_depth = slots // groups
    flat_shape = (slots * tile_size // 2, 2 * tile_size)
    targets = jnp.arange(groups, dtype=jnp.int32)[:, None]

    def local_lists(index_list, count_list, row_size, col_size):
        blocks = index_list.reshape(groups, bucket_depth, 2)
        rows_local = blocks[..., 0] - owner_index * row_size
        cols_local = blocks[..., 1] - targets * col_size
        valid_mask = (
            jnp.arange(bucket_depth, dtype=jnp.int32)[None, :] < count_list[:, None]
        ).astype(jnp.float32)
        return (rows_local, cols_local, valid_mask)

    gate_lists = local_lists(gate_index, gate_count, d_own, f_own)
    up_lists = local_lists(up_index, up_count, d_own, f_own)
    down_lists = local_lists(down_index, down_count, f_own, d_own)
    down_row, down_col = block_tables(down_lists[0], down_lists[1], down_lists[2], f_own, d_own)
    gate_blocks = gate_tiles.reshape(groups, bucket_depth, tile_size, tile_size)
    up_blocks = up_tiles.reshape(groups, bucket_depth, tile_size, tile_size)
    down_blocks = down_tiles.reshape(groups, bucket_depth, tile_size, tile_size)
    token_rows = tokens.reshape(tok_rows, d_own, tile_size)
    gate_row, gate_col = block_tables(gate_lists[0], gate_lists[1], gate_lists[2], d_own, f_own)
    up_row, up_col = block_tables(up_lists[0], up_lists[1], up_lists[2], d_own, f_own)
    gate_term = rounded(
        tile_forward(token_rows, gate_blocks, gate_row, gate_col).reshape(tok_rows, -1)
    )
    up_term = rounded(tile_forward(token_rows, up_blocks, up_row, up_col).reshape(tok_rows, -1))
    gate, up = (
        lax.psum_scatter(
            gate_term.astype(jnp.bfloat16), "mp", scatter_dimension=1, tiled=True
        ).astype(jnp.float32),
        lax.psum_scatter(
            up_term.astype(jnp.bfloat16), "mp", scatter_dimension=1, tiled=True
        ).astype(jnp.float32),
    )
    gate_three = gate.reshape(tok_rows, f_own, tile_size)
    up_three = up.reshape(tok_rows, f_own, tile_size)
    sigmoid_gate = jax.nn.sigmoid(gate_three)
    activated = gate_three * sigmoid_gate
    hidden = (activated * up_three).astype(jnp.bfloat16)
    down_term = rounded(tile_forward(hidden, down_blocks, down_row, down_col).reshape(tok_rows, -1))
    layer_output = lax.psum_scatter(
        down_term.astype(jnp.bfloat16), "mp", scatter_dimension=1, tiled=True
    )
    cotangent = lax.all_gather(grad_output, "mp", axis=1, tiled=True).reshape(
        tok_rows, groups, d_own, tile_size
    )
    grad_hidden = tile_backward(cotangent, down_blocks, down_row, down_col, True)
    grad_gate_pre = (
        grad_hidden * up_three * (sigmoid_gate * (1.0 + gate_three * (1.0 - sigmoid_gate)))
    ).astype(jnp.bfloat16)
    grad_up_pre = (grad_hidden * activated).astype(jnp.bfloat16)
    down_part = rounded(tile_grads(hidden, cotangent, down_row, down_col))
    group_span = f_own * tile_size
    piece_gate = lax.all_gather(grad_gate_pre.reshape(tok_rows, -1), "mp", axis=1, tiled=True)
    piece_up = lax.all_gather(grad_up_pre.reshape(tok_rows, -1), "mp", axis=1, tiled=True)
    count_groups = piece_gate.shape[1] // group_span
    gate_four = piece_gate.reshape(tok_rows, count_groups, f_own, tile_size)
    up_four = piece_up.reshape(tok_rows, count_groups, f_own, tile_size)
    contrib = tile_backward(gate_four, gate_blocks, gate_row, gate_col, False)
    contrib = contrib + tile_backward(up_four, up_blocks, up_row, up_col, False)
    running = rounded(contrib).sum(axis=1)
    gate_new = tile_grads(token_rows, gate_four, gate_row, gate_col)
    up_new = tile_grads(token_rows, up_four, up_row, up_col)
    gate_sum = gate_new
    up_sum = up_new
    running, gate_sum, up_sum = (running, gate_sum, up_sum)
    grad_tokens = running.reshape(tok_rows, -1).astype(jnp.bfloat16)
    summed = (
        lax.psum(rounded(gate_sum).astype(jnp.bfloat16), "dp").astype(jnp.float32),
        lax.psum(rounded(up_sum).astype(jnp.bfloat16), "dp").astype(jnp.float32),
        lax.psum(down_part.astype(jnp.bfloat16), "dp").astype(jnp.float32),
    )
    grad_gate = summed[0].astype(jnp.bfloat16).reshape(flat_shape)
    grad_up = summed[1].astype(jnp.bfloat16).reshape(flat_shape)
    grad_down = summed[2].astype(jnp.bfloat16).reshape(flat_shape)
    return (layer_output, grad_tokens, grad_gate, grad_up, grad_down)


def solution(mesh):
    return jax.shard_map(
        per_device,
        mesh=mesh,
        in_specs=(
            P("dp", "mp"),
            P("mp", None),
            P("mp", None),
            P("mp"),
            P("mp", None),
            P("mp", None),
            P("mp"),
            P("mp", None),
            P("mp", None),
            P("mp"),
            P("dp", "mp"),
        ),
        out_specs=(P("dp", "mp"), P("dp", "mp"), P("mp", None), P("mp", None), P("mp", None)),
        check_vma=False,
    )
```

profile of v0, /device:TPU:1, one launch (start us, length us, event | category | flops | bytes accessed | tf_op | source)
XLA Modules:
  0.0 444.9 jit_solution(17074445100574734331)
XLA Ops:
  7.2 1.7 copy.158
  9.0 0.8 reshape.170
  9.8 0.8 reshape.175
  10.6 0.7 fusion.89
  11.3 0.1 copy.181
  11.4 1.0 copy.135
  12.5 3.8 reshape.172
  16.5 0.7 convert_bitcast_fusion.8
  17.2 0.9 copy-done.7
  18.1 0.8 convolution_bitcast_fusion.5
  19.0 5.1 %convert_bitcast_fusion.1 = bf16[128,16,14,64]{0,2,3,1:T(8,128)(2,1)S(1)} fusion(f32[128,16,8,64]{0,3,2,1:T(8,128)S(1)} %convolution_bitcast_fusion.5, s32[16,8]{1,0:T(8,128)S(1)} %copy.133), kind=kOutput, calls=%fused_computation.18 | convolution fusion | flops 177997568 | bytes 7864832 | tf_op jit(solution)/shard_map/tgci,gcr->tgri/dot_general | solution.py:33
  24.1 2.8 copy.141
  26.9 0.6 copy-done.17
  27.5 0.1 copy.184
  27.6 0.5 copy-done.12
  28.1 1.8 reshape.176
  30.0 0.7 convert_bitcast_fusion.7
  30.7 1.4 copy-done
  32.1 0.8 convolution_bitcast_fusion.4
  32.9 5.1 %convert_bitcast_fusion = bf16[128,16,14,64]{0,2,3,1:T(8,128)(2,1)S(1)} fusion(f32[128,16,8,64]{0,3,2,1:T(8,128)S(1)} %convolution_bitcast_fusion.4, s32[16,8]{1,0:T(8,128)S(1)} %copy.143), kind=kOutput, calls=%fused_computation.17 | convolution fusion | flops 177997568 | bytes 7864832 | tf_op jit(solution)/shard_map/tgci,gcr->tgri/dot_general | solution.py:33
  38.1 2.8 copy.150
  40.9 9.4 %all-gather.6.cloned.1.call-start = ((), (), s32[]{:S(2)}) async-start(), calls=%async_computation.7 | async-start | bytes 3899392 | tf_op jit(solution)/shard_map/all_gather | solution.py:138
  50.6 1.8 reshape.179
  52.5 1.8 all-gather.4.cloned.1.call-done
  54.4 3.1 convert_bitcast_fusion.4
  57.5 0.7 convolution_bitcast_fusion.2
  58.2 0.6 copy-done.2
  58.8 6.2 %fusion.47 = f32[14,128,64]{1,0,2:T(8,128)S(1)} fusion(f32[128,16,8,64]{0,3,2,1:T(8,128)S(1)} %convolution_bitcast_fusion.2, f32[16,8,14]{0,1,2:T(8,128)S(1)} %fusion.73), kind=kOutput, calls=%fused_computation.50 | convolution fusion | flops 176160768 | bytes 4660224 | tf_op jit(solution)/shard_map/tgci,gcr->tri/dot_general | solution.py:33
  65.0 48.5 %reduce-scatter.4.cloned.1.call-done = bf16[128,896]{0,1:T(8,128)(2,1)} async-done(((bf16[128,14336]{0,1:T(8,128)(2,1)}), bf16[128,896]{0,1:T(8,128)(2,1)}) %reduce-scatter.4.cloned.1.call-update) | async-done | bytes 229392 | tf_op jit(solution)/shard_map/reduce_scatter | solution.py:112
  113.5 62.9 %reduce-scatter.6.cloned.1.call-done = bf16[128,896]{0,1:T(8,128)(2,1)} async-done(((bf16[128,14336]{0,1:T(8,128)(2,1)}), bf16[128,896]{0,1:T(8,128)(2,1)}) %reduce-scatter.6.cloned.1.call-update) | async-done | bytes 229392 | tf_op jit(solution)/shard_map/reduce_scatter | solution.py:115
  176.4 2.2 fusion.52
  178.7 0.5 all-gather.8.cloned.1.call-update
  179.3 0.1 copy.187
  179.5 0.7 convert_bitcast_fusion.6
  180.2 0.9 copy-done.11
  181.0 0.8 convolution_bitcast_fusion.3
  181.9 0.5 copy-done.6
  182.3 4.0 convert_bitcast_fusion.5
  186.3 1.9 copy.157
  188.3 0.3 all-reduce.3.cloned.1.call-start
  188.5 4.8 %convolution_convert_fusion = bf16[16,8,64,64]{3,2,1,0:T(8,128)(2,1)} fusion(bf16[128,16,8,64]{0,2,3,1:T(8,128)(2,1)} %copy-done.2, bf16[128,16,8,64]{0,2,3,1:T(8,128)(2,1)} %copy-done.6), kind=kOutput, calls=%fused_computation.34 | convolution fusion | flops 134742016 | bytes 5242880 | tf_op jit(solution)/shard_map/tgci,tgcj->gcij/dot_general | solution.py:51
  193.3 3.9 reshape.187
  197.2 25.3 %all-gather.6.cloned.1.call-done = bf16[128,14336]{0,1:T(8,128)(2,1)} async-done(((bf16[128,896]{0,1:T(8,128)(2,1)}), bf16[128,14336]{0,1:T(8,128)(2,1)}) %all-gather.6.cloned.1.call-update) | async-done | bytes 3670032 | tf_op jit(solution)/shard_map/all_gather | solution.py:138
  222.5 4.2 convert_bitcast_fusion.3
  226.7 1.3 copy-done.3
  228.0 2.5 convolution_convert_fusion.2
  230.6 3.9 reshape.185
  234.5 30.5 %all-gather.8.cloned.1.call-done = bf16[128,14336]{0,1:T(8,128)(2,1)} async-done(((bf16[128,896]{0,1:T(8,128)(2,1)}), bf16[128,14336]{0,1:T(8,128)(2,1)}) %all-gather.8.cloned.1.call-update) | async-done | bytes 3670032 | tf_op jit(solution)/shard_map/all_gather | solution.py:139
  265.0 4.4 convert_bitcast_fusion.2
  269.4 1.4 copy-done.5
  270.7 2.6 convolution_convert_fusion.1
  273.3 4.1 reshape.186
  277.7 44.1 %reduce-scatter.8.cloned.1.call-done = bf16[128,512]{0,1:T(8,128)(2,1)} async-done(((bf16[128,8192]{0,1:T(8,128)(2,1)}), bf16[128,512]{0,1:T(8,128)(2,1)}) %reduce-scatter.8.cloned.1.call-update) | async-done | bytes 131088 | tf_op jit(solution)/shard_map/reduce_scatter | solution.py:125
  321.8 1.7 copy.179
  323.4 3.1 convolution_bitcast_fusion
  326.5 0.4 copy-done.8
  326.9 0.7 convolution_bitcast_fusion.1
  327.6 6.2 %fusion = f32[16,8,128,64]{2,1,3,0:T(8,128)S(1)} fusion(f32[16,8,8,1]{1,2,3,0:T(8,128)S(1)} %copy.195, f32[128,16,8,64]{0,3,2,1:T(8,128)S(1)} %convolution_bitcast_fusion), kind=kOutput, calls=%fused_computation | convolution fusion | flops 100663296 | bytes 8392704 | tf_op jit(solution)/shard_map/tgci,gcr->tgri/dot_general | solution.py:33
  333.9 7.8 %fusion.44 = bf16[8,128,64]{1,0,2:T(8,128)(2,1)S(1)} fusion(f32[16,8,128,64]{2,1,3,0:T(8,128)S(1)} %fusion, f32[16,8,8,1]{1,2,3,0:T(8,128)S(1)} %copy.193, f32[128,16,8,64]{0,3,2,1:T(8,128)S(1)} %convolution_bitcast_fusion.1), kind=kOutput, calls=%fused_computation.49 | convolution fusion | flops 103743488 | bytes 8523776 | tf_op jit(solution)/shard_map/tgci,gcr->tgri/dot_general | solution.py:33
  341.6 0.8 copy.180
  342.4 90.8 %all-reduce.3.cloned.1.call-done = (bf16[4096,128]{1,0:T(8,128)(2,1)}, bf16[4096,128]{1,0:T(8,128)(2,1)}, bf16[4096,128]{1,0:T(8,128)(2,1)}) async-done(((bf16[4096,128]{1,0:T(8,128)(2,1)}, bf16[4096,128]{1,0:T(8,128)(2,1)}, bf16[4096,128]{1,0:T(8,128)(2,1)}), (bf16[4096,128]{1,0:T(8,128)(2,1)}, bf16[4096,128]{1,0:T(8,128)(2,1)}, bf16[4096,128]{1,0:T(8,128)(2,1)})) %all-reduce.3.cloned.1.call-update) | async-done | bytes 3145744 | tf_op jit(solution)/shard_map/psum | solution.py:153
  433.2 2.4 copy.295
  435.6 1.0 copy.296
  436.6 1.0 copy.297
  (69 shorter events, 1.4 us)
Async XLA Ops:
  7.2 47.2 %all-gather.4.cloned.1.call-start = ((), (), s32[]{:S(2)}) async-start(), calls=%async_computation.6 | async-start | bytes 2228224 | tf_op jit(solution)/shard_map/all_gather | solution.py:128
  8.9 104.6 %reduce-scatter.4.cloned.1.call-start = ((), (), s32[]{:S(2)}) async-start(), calls=%async_computation.3 | async-start | bytes 3899392 | tf_op jit(solution)/shard_map/reduce_scatter | solution.py:112
  16.5 1.6 copy-start.7
  26.9 0.7 copy-start.17
  26.9 1.2 copy-start.12
  26.9 149.6 %reduce-scatter.6.cloned.1.call-start = ((), (), s32[]{:S(2)}) async-start(), calls=%async_computation.4 | async-start | bytes 3899392 | tf_op jit(solution)/shard_map/reduce_scatter | solution.py:115
  30.0 2.1 copy-start.9
  30.7 1.4 copy-start
  40.9 9.5 %copy-start.16 = (s32[128,2]{0,1:T(2,128)S(1)}, s32[128,2]{0,1:T(2,128)}, u32[]{:S(2)}) copy-start(s32[128,2]{0,1:T(2,128)} %param.19) | copy-start | bytes 3076
  40.9 9.8 %copy-start.13 = (bf16[4096,128]{1,0:T(8,128)(2,1)S(1)}, bf16[4096,128]{1,0:T(8,128)(2,1)}, u32[]{:S(2)}) copy-start(bf16[4096,128]{1,0:T(8,128)(2,1)} %param.18) | copy-start | bytes 3145732
  40.9 11.6 %copy-start.18 = (s32[16]{0:T(128)S(1)}, s32[16]{0:T(128)}, u32[]{:S(2)}) copy-start(s32[16]{0:T(128)} %param.20) | copy-start | bytes 196
  40.9 181.6 %all-gather.6.cloned.1.call-start = ((), (), s32[]{:S(2)}) async-start(), calls=%async_computation.7 | async-start | bytes 3899392 | tf_op jit(solution)/shard_map/all_gather | solution.py:138
  54.4 3.1 copy-start.10
  57.5 1.3 copy-start.2
  178.6 86.3 %all-gather.8.cloned.1.call-start = ((), (), s32[]{:S(2)}) async-start(), calls=%async_computation.8 | async-start | bytes 3899392 | tf_op jit(solution)/shard_map/all_gather | solution.py:139
  179.2 142.5 %reduce-scatter.8.cloned.1.call-start = ((), (), s32[]{:S(2)}) async-start(), calls=%async_computation.5 | async-start | bytes 2228224 | tf_op jit(solution)/shard_map/reduce_scatter | solution.py:125
  179.4 1.6 copy-start.11
  181.0 1.3 copy-start.6
  188.3 245.0 %all-reduce.3.cloned.1.call-start = ((), (), s32[]{:S(2)}) async-start(), calls=%async_computation.9 | async-start | bytes 6291456 | tf_op jit(solution)/shard_map/psum | solution.py:153
  226.7 1.3 copy-start.3
  265.0 5.7 %copy-start.1 = (bf16[128,16,8,64]{0,2,3,1:T(8,128)(2,1)S(1)}, bf16[128,16,8,64]{0,2,3,1:T(8,128)(2,1)}, u32[]{:S(2)}) copy-start(bf16[128,16,8,64]{0,2,3,1:T(8,128)(2,1)} %copy-done) | copy-start | bytes 6291460
  269.3 1.4 copy-start.5
  323.4 3.1 copy-start.4
  323.4 3.5 copy-start.8
  433.2 2.4 copy-start.15
  433.2 3.4 copy-start.14
Sparse Core Ops, SparseCore 0:
  10.4 43.9 all-gather.3
  57.0 56.5 reduce-scatter.3
  116.1 60.3 reduce-scatter.5
  178.8 43.6 all-gather.5
  224.8 40.1 all-gather.7
  267.4 54.3 reduce-scatter.7
  326.0 107.1 all-reduce.2
where the time goes:
time: 454 us; the launch traced here: 445 us
  waiting for transfers between devices  305 us (67%)
  matrix products  65.1 us (14%)
  local copies, waits for them, and re-layouts  47.5 us (10%)
  between operations  14.9 us (3%)
  starting transfers between devices  9.9 us (2%)
    psum x1, waiting for transfers between devices, per_device(): lax.psum(rounded(gate_sum).astype(jnp.bfloat16), 'dp').astype(jnp.float32)  90.8 us
    reduce_scatter x1, waiting for transfers between devices, per_device(): lax.psum_scatter(up_term.astype(jnp.bfloat16), 'mp', scatter_dimension=1,...  62.9 us
    reduce_scatter x1, waiting for transfers between devices, per_device(): lax.psum_scatter(gate_term.astype(jnp.bfloat16), 'mp', scatter_dimension=...  48.5 us
    reduce_scatter x1, waiting for transfers between devices, per_device(): lax.psum_scatter(down_term.astype(jnp.bfloat16), 'mp', scatter_dimension=...  44.1 us
    dot_general x6, matrix products, place_blocks(): return jnp.einsum(form, product, hot_table, precision=HIGH)  34.4 us
    all_gather x1, waiting for transfers between devices, per_device(): lax.all_gather(grad_up_pre.reshape(tok_rows, -1), 'mp', axis=1, tiled=True)  30.5 us
    all_gather x1, waiting for transfers between devices, per_device(): lax.all_gather(grad_gate_pre.reshape(tok_rows, -1), 'mp', axis=1, tiled=T...  25.3 us
    unnamed x51, local copies, waits for them, and re-layouts  18.3 us
  transfers between devices with their start and end apart: 7, of which 7 were waited for; matrix products, arithmetic and copies ran while one was open for 22% of the time, Pallas kernels for 0%

commit v1 on v0

v1 whole, which is shorter than its diff:
```python
import jax
import jax.numpy as jnp
from jax import lax
from jax.experimental import pallas as pl
from jax.experimental.pallas import tpu as pltpu
from jax.sharding import PartitionSpec as P

FF = 14336
TILE = 64
HALF = TILE // 2
DEPTH = 8
D_OWN = 8
F_OWN = 14
GROUPS = 16
SIDE = 4
CHUNKS = 4
BF = jnp.bfloat16
F32 = jnp.float32


def tn(a, b):
    return lax.dot_general(a, b, (((0,), (0,)), ((), ())), preferred_element_type=F32)


def nn(a, b):
    return lax.dot_general(a, b, (((1,), (0,)), ((), ())), preferred_element_type=F32)


def nt(a, b):
    return lax.dot_general(a, b, (((1,), (1,)), ((), ())), preferred_element_type=F32)


def unpack(tile):
    return jnp.concatenate([tile[:, :TILE], tile[:, TILE:]], axis=0)


def pack(values):
    return jnp.concatenate([values[:HALF], values[HALF:]], axis=1)


def down_kernel(dmeta, act, down, grad_hidden, down_t, cot, acc, sems):
    span = GROUPS // CHUNKS
    copies = [
        pltpu.make_async_copy(
            act.at[pl.ds(n * span, span), 1], cot.at[pl.ds(n * span, span)], sems.at[n]
        )
        for n in range(CHUNKS)
    ]
    for copy in copies:
        copy.start()
    for f in range(F_OWN):
        acc[f] = jnp.zeros((TILE, 128), F32)

    for n in range(CHUNKS):
        copies[n].wait()

        @pl.loop(n * span, (n + 1) * span, unroll=span)
        def _(e):
            tiles = [unpack(down[e * DEPTH + c]) for c in range(DEPTH)]
            parts = [nn(tiles[c], cot[e, dmeta[1, e * DEPTH + c]]) for c in range(DEPTH)]
            for c in range(DEPTH):
                acc[dmeta[0, e * DEPTH + c]] += parts[c]

    @pl.loop(0, GROUPS, unroll=2)
    def _(e):
        for c in range(DEPTH):
            down_t[e * DEPTH + c] = unpack(down[e * DEPTH + c]).T

    for f in range(F_OWN):
        grad_hidden[f, pl.ds(0, HALF, stride=2), :] = acc[f, :HALF]
        grad_hidden[f, pl.ds(1, HALF, stride=2), :] = acc[f, HALF:]


def layer_kernel(
    meta,
    dmeta,
    act,
    gu,
    grad_hidden,
    grads,
    hidden_split,
    pre,
    pairs,
    tiles,
    tokens,
    cot,
    grads_v,
    acc,
    strided,
    sems,
):
    span = GROUPS // CHUNKS

    def loads(n):
        rows = pl.ds(n * span, span)
        return (
            pltpu.make_async_copy(act.at[rows, 2], pairs.at[rows], sems.at[0, n]),
            pltpu.make_async_copy(gu.at[:, rows], tiles.at[:, rows], sems.at[1, n]),
        )

    first = [loads(n) for n in range(CHUNKS)]
    load_tokens = pltpu.make_async_copy(act.at[:, 0], tokens, sems.at[2, 0])
    load_cot = pltpu.make_async_copy(act.at[:, 1], cot, sems.at[2, 1])
    store = pltpu.make_async_copy(grads_v, grads, sems.at[2, 2])
    for pair in first:
        for copy in pair:
            copy.start()
    load_tokens.start()
    load_cot.start()
    for f in range(2 * F_OWN):
        acc[f] = jnp.zeros((128, TILE), F32)

    for n in range(CHUNKS):
        for copy in first[n]:
            copy.wait()

        @pl.loop(n * span, (n + 1) * span, unroll=span)
        def _(q):
            for base in range(0, 2 * DEPTH, 4):
                parts = []
                for m in range(base, base + 4):
                    tile = unpack(tiles[m, q])
                    row = meta[q, m]
                    odd = jnp.broadcast_to(row % 2, tile.shape) > 0
                    none = jnp.zeros_like(tile)
                    tall = jnp.concatenate(
                        [jnp.where(odd, none, tile), jnp.where(odd, tile, none)], axis=0
                    )
                    pair = 2 * (row // 2)
                    both = jnp.concatenate([pairs[q, pair], pairs[q, pair + 1]], axis=0)
                    parts.append(nn(both, tall))
                for m in range(base, base + 4):
                    acc[meta[q, 2 * DEPTH + m]] += parts[m - base]

    for f in range(F_OWN):
        back = grad_hidden[f]
        gate = acc[f].T
        up = acc[F_OWN + f].T
        sig = jax.nn.sigmoid(gate)
        activated = gate * sig
        pre[f] = (back * up * (sig * (1.0 + gate * (1.0 - sig)))).astype(BF)
        pre[F_OWN + f] = (back * activated).astype(BF)
        strided[f] = activated * up
        hidden_split[f, :HALF] = strided[f, pl.ds(0, HALF, stride=2), :].astype(BF)
        hidden_split[f, HALF:] = strided[f, pl.ds(1, HALF, stride=2), :].astype(BF)

    load_tokens.wait()

    @pl.loop(0, GROUPS, unroll=8)
    def _(q):
        for m in range(2 * DEPTH):
            got = nt(tokens[q, meta[q, m]], pre[meta[q, 2 * DEPTH + m]])
            grads_v[m, q] = pack(got.astype(BF))

    load_cot.wait()

    @pl.loop(0, GROUPS, unroll=8)
    def _(q):
        for c in range(DEPTH):
            k = q * DEPTH + c
            got = nt(hidden_split[dmeta[0, k]], cot[q, dmeta[1, k]])
            live = jnp.broadcast_to(dmeta[2, k], got.shape) > 0
            grads_v[q, GROUPS + c] = pack(jnp.where(live, got, 0.0).astype(BF))

    store.start()
    store.wait()


def output_kernel(meta, dmeta, gu, down_t, hidden_split, pre, partials, tiles, turned, sums, acc, sems):
    span = GROUPS // CHUNKS
    zero_block = jnp.zeros((TILE, 128), F32)

    def loads(n):
        rows = pl.ds(n * span, span)
        flat = pl.ds(n * span * DEPTH, span * DEPTH)
        return (
            pltpu.make_async_copy(gu.at[:, rows], tiles.at[:, rows], sems.at[0, n]),
            pltpu.make_async_copy(down_t.at[flat], turned.at[flat], sems.at[1, n]),
        )

    def store(n):
        rows = pl.ds(n * span, span)
        return pltpu.make_async_copy(sums.at[rows], partials.at[rows], sems.at[2, n])

    first = [loads(n) for n in range(CHUNKS)]
    for pair in first:
        for copy in pair:
            copy.start()

    for n in range(CHUNKS):
        for copy in first[n]:
            copy.wait()

        @pl.loop(n * span, (n + 1) * span, unroll=span)
        def _(q):
            for r in range(D_OWN):
                acc[0, r] = zero_block
                acc[1, r] = zero_block
            for base in range(0, DEPTH, 4):
                parts = []
                for c in range(base, base + 4):
                    k = q * DEPTH + c
                    parts.append(nn(turned[k], hidden_split[dmeta[0, k]]))
                for c in range(base, base + 4):
                    acc[0, dmeta[1, q * DEPTH + c]] += parts[c - base]
            for base in range(0, 2 * DEPTH, 4):
                parts = []
                for m in range(base, base + 4):
                    parts.append(nn(unpack(tiles[m, q]), pre[meta[q, 2 * DEPTH + m]]))
                for m in range(base, base + 4):
                    acc[1, meta[q, m]] += parts[m - base]
            for r in range(D_OWN):
                sums[q, 0, r] = acc[0, r].astype(BF)
                sums[q, 1, r] = acc[1, r].astype(BF)

        store(n).start()
    for n in range(CHUNKS):
        store(n).wait()


SMEM = pl.BlockSpec(memory_space=pltpu.SMEM)
VMEM = pl.BlockSpec(memory_space=pltpu.VMEM)
ANY = pl.BlockSpec(memory_space=pl.ANY)
LIMIT = 48 * 1024 * 1024


def down_part(dmeta, act, down):
    return pl.pallas_call(
        down_kernel,
        out_shape=(
            jax.ShapeDtypeStruct((F_OWN, TILE, 128), F32),
            jax.ShapeDtypeStruct((GROUPS * DEPTH, TILE, TILE), BF),
        ),
        in_specs=[SMEM, ANY, VMEM],
        out_specs=(VMEM, VMEM),
        scratch_shapes=[
            pltpu.VMEM((GROUPS, D_OWN, TILE, 128), BF),
            pltpu.VMEM((F_OWN, TILE, 128), F32),
            pltpu.SemaphoreType.DMA((CHUNKS,)),
        ],
        compiler_params=pltpu.CompilerParams(vmem_limit_bytes=LIMIT),
        cost_estimate=pl.CostEstimate(flops=2**27, bytes_accessed=2**23, transcendentals=0),
        name="down_kernel",
    )(dmeta, act, down)


def layer(meta, dmeta, act, gu, grad_hidden):
    block = (GROUPS, D_OWN, TILE, 128)
    return pl.pallas_call(
        layer_kernel,
        out_shape=(
            jax.ShapeDtypeStruct((GROUPS, 3 * DEPTH, HALF, 128), BF),
            jax.ShapeDtypeStruct((F_OWN, TILE, 128), BF),
            jax.ShapeDtypeStruct((2 * F_OWN, TILE, 128), BF),
        ),
        in_specs=[SMEM, SMEM, ANY, ANY, VMEM],
        out_specs=(ANY, VMEM, VMEM),
        scratch_shapes=[
            pltpu.VMEM(block, BF),
            pltpu.VMEM((2 * DEPTH, GROUPS, HALF, 128), BF),
            pltpu.VMEM(block, BF),
            pltpu.VMEM(block, BF),
            pltpu.VMEM((GROUPS, 3 * DEPTH, HALF, 128), BF),
            pltpu.VMEM((2 * F_OWN, 128, TILE), F32),
            pltpu.VMEM((F_OWN, TILE, 128), F32),
            pltpu.SemaphoreType.DMA((3, CHUNKS)),
        ],
        compiler_params=pltpu.CompilerParams(vmem_limit_bytes=LIMIT),
        cost_estimate=pl.CostEstimate(flops=2**29, bytes_accessed=2**23, transcendentals=0),
        name="layer_kernel",
    )(meta, dmeta, act, gu, grad_hidden)


def output_part(meta, dmeta, gu, down_t, hidden_split, pre):
    return pl.pallas_call(
        output_kernel,
        out_shape=jax.ShapeDtypeStruct((GROUPS, 2, D_OWN, TILE, 128), BF),
        in_specs=[SMEM, SMEM, ANY, ANY, VMEM, VMEM],
        out_specs=ANY,
        scratch_shapes=[
            pltpu.VMEM((2 * DEPTH, GROUPS, HALF, 128), BF),
            pltpu.VMEM((GROUPS * DEPTH, TILE, TILE), BF),
            pltpu.VMEM((GROUPS, 2, D_OWN, TILE, 128), BF),
            pltpu.VMEM((2, D_OWN, TILE, 128), F32),
            pltpu.SemaphoreType.DMA((3, CHUNKS)),
        ],
        compiler_params=pltpu.CompilerParams(vmem_limit_bytes=LIMIT),
        cost_estimate=pl.CostEstimate(flops=2**28, bytes_accessed=2**23, transcendentals=0),
        name="output_kernel",
    )(meta, dmeta, gu, down_t, hidden_split, pre)


def split_order(size):
    n = jnp.arange(size, dtype=jnp.int32)
    block, inner = n // TILE, n % TILE
    source = block * TILE + 2 * (inner % HALF) + inner // HALF
    return (source[:, None] == n[None, :]).astype(BF)


def lines(second):
    groups = []
    for mp in range(GROUPS):
        for other in range(SIDE):
            along_x = (mp % 2 == 0) != second
            groups.append(
                [
                    ((n * SIDE + other) if along_x else (other * SIDE + n)) * GROUPS + mp
                    for n in range(SIDE)
                ]
            )
    return groups


def exchange(parts, second):
    return lax.all_to_all(
        parts, ("dp", "mp"), 0, 0, tiled=True, axis_index_groups=lines(second)
    )


def spread(piece, second):
    return exchange(jnp.broadcast_to(piece[None], (SIDE,) + piece.shape), second)


def to_replicas(piece):
    got = spread(spread(piece, True), False)
    return got.reshape((GROUPS,) + piece.shape)


def from_replicas(parts):
    parts = parts.reshape((SIDE, SIDE) + parts.shape[1:])
    for second in (False, True):
        parts = exchange(parts, second).astype(F32).sum(axis=0).astype(BF)
    return parts


def per_device(
    tokens,
    gate_tiles,
    gate_index,
    gate_count,
    up_tiles,
    up_index,
    up_count,
    down_tiles,
    down_index,
    down_count,
    grad_output,
):
    me = lax.axis_index("mp")
    replica = lax.axis_index("dp")
    crossed = me % 2
    turned = (replica % SIDE) * SIDE + replica // SIDE
    part = jnp.where(crossed == 1, turned, replica)
    width = tokens.shape[1]
    order = split_order(width)
    eye = jnp.eye(width, dtype=BF)
    groups = jnp.arange(GROUPS, dtype=jnp.int32)[:, None]
    slots = jnp.arange(DEPTH, dtype=jnp.int32)[None, :]

    tokens_t = jnp.einsum("pi,ti->pt", order, tokens, preferred_element_type=F32).astype(BF)
    grad_t = jnp.einsum("pi,ti->pt", eye, grad_output, preferred_element_type=F32).astype(BF)
    tokens_p = jnp.einsum("ti,pi->tp", tokens, order, preferred_element_type=F32).astype(BF)
    tokens_p = tokens_p.reshape(128, width // 128, 128).transpose(1, 0, 2).reshape(width, 128)
    own = jnp.concatenate([tokens_t, grad_t, tokens_p], axis=0)
    own, gate_index, up_index, gate_tiles, up_tiles = lax.optimization_barrier(
        (own, gate_index, up_index, gate_tiles, up_tiles)
    )
    act = lax.all_gather(own, "mp", axis=0)
    act = act.reshape(GROUPS, 3, D_OWN, TILE, 128)

    def blocks(index):
        return index.reshape(GROUPS, DEPTH, 2)

    is_up = part // DEPTH
    depth = part % DEPTH
    gate_t = lax.dynamic_index_in_dim(
        gate_tiles.reshape(GROUPS, DEPTH, HALF, 128), depth, 1, keepdims=False
    )
    up_t = lax.dynamic_index_in_dim(
        up_tiles.reshape(GROUPS, DEPTH, HALF, 128), depth, 1, keepdims=False
    )
    count = jnp.where(is_up == 1, up_count, gate_count)
    my_live = (depth < count)[:, None, None]
    mine = jnp.where(my_live, jnp.where(is_up == 1, up_t, gate_t), 0)
    gate_b, up_b = blocks(gate_index), blocks(up_index)
    notes = jnp.concatenate(
        [
            gate_b[..., 0] - me * D_OWN,
            up_b[..., 0] - me * D_OWN,
            gate_b[..., 1] - groups * F_OWN,
            up_b[..., 1] - groups * F_OWN + F_OWN,
        ],
        axis=1,
    ).astype(BF)
    notes = jnp.pad(notes[:, None, :], ((0, 0), (0, 7), (0, 128 - 4 * DEPTH)))
    sent = lax.all_to_all(
        jnp.concatenate([mine, notes], axis=1), "mp", 0, 0, tiled=True
    )
    meta = sent[:, HALF, : 4 * DEPTH].astype(jnp.int32).reshape(GROUPS, 2, SIDE, SIDE)
    same = (groups % 2 == crossed)[..., None, None]
    meta = jnp.where(same, meta, meta.swapaxes(2, 3)).reshape(GROUPS, 4 * DEPTH)
    gu = to_replicas(sent[:, :HALF])

    down_b = blocks(down_index)
    down_live = slots < down_count[:, None]
    dmeta = jnp.stack(
        [
            (down_b[..., 0] - me * F_OWN).reshape(-1),
            (down_b[..., 1] - groups * D_OWN).reshape(-1),
            down_live.astype(jnp.int32).reshape(-1),
        ]
    )
    down = jnp.where(
        down_live.reshape(-1)[:, None, None], down_tiles.reshape(GROUPS * DEPTH, HALF, 128), 0
    )

    grad_hidden, down_t = down_part(dmeta, act, down)
    grads, hidden_split, pre = layer(meta, dmeta, act, gu, grad_hidden)
    partials = output_part(meta, dmeta, gu, down_t, hidden_split, pre)

    summed = lax.psum_scatter(
        partials.reshape(GROUPS * 2 * width, 128), "mp", scatter_dimension=0, tiled=True
    )
    layer_output = jnp.einsum(
        "pt,pi->ti", summed[:width], eye, preferred_element_type=F32
    ).astype(BF)
    grad_tokens = jnp.einsum(
        "pt,pi->ti", summed[width:], order, preferred_element_type=F32
    ).astype(BF)

    got = from_replicas(grads)
    back = lax.all_to_all(got[:GROUPS], "mp", 0, 0, tiled=True)
    piece = jnp.concatenate([jnp.where(my_live, back, 0), got[GROUPS:]], axis=0)
    full = to_replicas(piece)
    flat = (GROUPS * DEPTH * HALF, 128)
    grad_gate = full[:DEPTH, :GROUPS].transpose(1, 0, 2, 3).reshape(flat)
    grad_up = full[DEPTH:, :GROUPS].transpose(1, 0, 2, 3).reshape(flat)
    grad_down = full[:, GROUPS:].reshape(flat)
    return (layer_output, grad_tokens, grad_gate, grad_up, grad_down)


def solution(mesh):
    return jax.shard_map(
        per_device,
        mesh=mesh,
        in_specs=(
            P("dp", "mp"),
            P("mp", None),
            P("mp", None),
            P("mp"),
            P("mp", None),
            P("mp", None),
            P("mp"),
            P("mp", None),
            P("mp", None),
            P("mp"),
            P("dp", "mp"),
        ),
        out_specs=(P("dp", "mp"), P("dp", "mp"), P("mp", None), P("mp", None), P("mp", None)),
        check_vma=False,
    )
```

time: 454 us -> 198 us (0.44); the launches traced: 445 us -> 198 us
  waiting for transfers between devices: 305 us -> 16.9 us
  blocking collectives: 0 us -> 105 us
  matrix products: 65.1 us -> 5.36 us
  local copies, waits for them, and re-layouts: 47.5 us -> 14 us
  Pallas kernels: 0 us -> 24.2 us
    reduce_scatter x3 -> x1, waiting for transfers between devices: 155 us -> 0.01 us  [per_device(): lax.psum_scatter(partials.reshape(GROUPS * 2 * width, 128), 'mp', scatter...]
    all_to_all x0 -> x6, blocking collectives: none -> 105 us  [the longest x5 84.5 us: exchange(): lax.all_to_all(parts, ('dp', 'mp'), 0, 0, tiled=True, axis_index_groups=l...]
    psum x1 -> x0, waiting for transfers between devices: 90.8 us -> none  [per_device(): lax.psum(rounded(gate_sum).astype(jnp.bfloat16), 'dp').astype(jnp.float32)]
    dot_general x21 -> x4, matrix products: 65.1 us -> 5.36 us  [the longest x1 1.98 us: per_device(): jnp.einsum('pt,pi->ti', summed[width:], order, preferred_element_type=F32)]
    all_gather x3 -> x1, waiting for transfers between devices: 57.7 us -> 8.33 us  [per_device(): act = lax.all_gather(own, 'mp', axis=0)]
    pallas_call x0 -> x3, Pallas kernels: none -> 24.2 us  [the longest x1 11.5 us: layer(): pl.pallas_call(layer_kernel, out_shape=(jax.ShapeDtypeStruct((GROUPS, 3 *...]
    reshape x9 -> x5, local copies, waits for them, and re-layouts: 21 us -> 1.81 us  [the longest x3 1.61 us: blocks(): return index.reshape(GROUPS, DEPTH, 2)]
    unnamed x51 -> x16, local copies, waits for them, and re-layouts: 18.3 us -> 4.1 us
  transfers between devices with their start and end apart: 7 -> 4, of which waited for: 7 -> 2; matrix products, arithmetic and copies ran while one was open for 22% -> 8% of each run, Pallas kernels for 0% -> 3%
where the time goes in v1:
time: 198 us
  blocking collectives  105 us (53%)
  Pallas kernels  24.2 us (12%)
  waiting for transfers between devices  16.9 us (9%)
  between operations  14.4 us (7%)
  local copies, waits for them, and re-layouts  14 us (7%)
  starting transfers between devices  11.4 us (6%)
  other arithmetic  6.06 us (3%)
  matrix products  5.36 us (3%)
    all_to_all x5, blocking collectives, exchange(): lax.all_to_all(parts, ('dp', 'mp'), 0, 0, tiled=True, axis_index_groups=l...  84.5 us
    all_to_all x1, blocking collectives, per_device(): lax.all_to_all(jnp.concatenate([mine, notes], axis=1), 'mp', 0, 0, tiled=...  20.9 us
    pallas_call x1, Pallas kernels, layer(): pl.pallas_call(layer_kernel, out_shape=(jax.ShapeDtypeStruct((GROUPS, 3 *...  11.5 us
    all_to_all x1, waiting for transfers between devices, per_device(): back = lax.all_to_all(got[:GROUPS], 'mp', 0, 0, tiled=True)  8.56 us
    all_gather x1, waiting for transfers between devices, per_device(): act = lax.all_gather(own, 'mp', axis=0)  8.33 us
    all_to_all x1, starting transfers between devices, per_device(): back = lax.all_to_all(got[:GROUPS], 'mp', 0, 0, tiled=True)  7.36 us
    pallas_call x1, Pallas kernels, output_part(): pl.pallas_call(output_kernel, out_shape=jax.ShapeDtypeStruct((GROUPS, 2,...  6.37 us
    pallas_call x1, Pallas kernels, down_part(): pl.pallas_call(down_kernel, out_shape=(jax.ShapeDtypeStruct((F_OWN, TILE,...  6.35 us
  transfers between devices with their start and end apart: 4, of which 2 were waited for; matrix products, arithmetic and copies ran while one was open for 8% of the time, Pallas kernels for 3%

profile of v1, /device:TPU:1, one launch (start us, length us, event | category | flops | bytes accessed | tf_op | source)
XLA Modules:
  0.0 197.8 jit_solution(16348529887243574496)
XLA Ops:
  7.2 0.0 copy-start
  7.2 0.0 all-gather.3.cloned.1.call-start
  7.2 0.8 copy-done
  8.1 0.4 convolution_convert_fusion.3
  8.4 0.1 copy.86
  8.6 1.2 convolution_convert_fusion.2
  9.8 0.8 pad_maximum_fusion
  10.6 0.0 all-gather.3.cloned.1.call-update
  10.7 0.8 reshape.322
  11.4 0.1 copy.102
  11.5 0.1 copy.89
  11.6 0.8 reshape.323
  12.3 0.1 copy.103
  12.4 0.1 copy.90
  12.5 0.1 copy.93
  12.6 0.1 copy.91
  12.7 0.1 copy.94
  12.8 0.1 copy.92
  12.9 0.1 fusion.12
  13.0 0.7 fusion.36
  13.7 1.1 bitcast_select_fusion
  14.7 20.9 %all_to_all.40 = bf16[16,40,128]{2,1,0:T(8,128)(2,1)S(1)} all-to-all(bf16[16,40,128]{2,1,0:T(8,128)(2,1)S(1)} %pad_maximum_fusion.2), channel_id=1, replica_groups=mesh['dp'=16,'mp'=16] {'mp'}, dimensions={0} | all-to-all | bytes 327680 | tf_op jit(solution)/shard_map/all_to_all | solution.py:396
  35.7 0.1 broadcast_in_dim.71
  35.8 11.1 %all_to_all.41 = bf16[4,16,32,128]{3,2,1,0:T(8,128)(2,1)S(1)} all-to-all(bf16[4,16,32,128]{3,2,1,0:T(8,128)(2,1)S(1)} %broadcast_in_dim.71), channel_id=1, replica_groups={{0,16,32,48},{64,80,96,112},{128,144,160,176},{192,208,224,240},{1,65,1..., dimensions={0} | all-to-all | bytes 1048576 | tf_op jit(solution)/shard_map/all_to_all | solution.py:315
  46.9 1.8 broadcast_in_dim.72
  48.6 4.0 %all-to-all-start.2 = ((bf16[4,4,16,32,128]{4,3,2,1,0:T(8,128)(2,1)}), bf16[4,4,16,32,128]{4,3,2,1,0:T(8,128)(2,1)S(1)}, u32[]{:S(2)}, u32[]{:S(2)}) async-start(bf16[4,4,16,32,128]{4,3,2,1,0:T(8,128)(2,1)} %broadcast_in_dim.72), calls=%async_computation.2 | async-start | bytes 4194304 | tf_op jit(solution)/shard_map/all_to_all | solution.py:315
  52.7 0.1 sub.119
  52.7 0.1 sub.120
  52.8 0.1 iota_compare_fusion.8
  52.9 0.1 lt.85
  53.0 0.1 reshape.336
  53.1 0.1 reshape.325
  53.2 0.1 sub.118
  53.3 0.1 squeeze.18
  53.4 1.4 broadcast_select_fusion.down
  54.9 0.1 copy.96
  55.0 0.1 copy.99.meta
  55.1 8.3 %all-gather.3.cloned.1.call-done = bf16[24576,128]{1,0:T(8,128)(2,1)} async-done(((bf16[1536,128]{1,0:T(8,128)(2,1)}), bf16[24576,128]{1,0:T(8,128)(2,1)}) %all-gather.3.cloned.1.call-update) | async-done | bytes 6291472 | tf_op jit(solution)/shard_map/all_gather | solution.py:368
  63.4 6.3 %down_kernel.1 = (f32[14,64,128]{2,1,0:T(8,128)S(1)}, bf16[128,64,64]{2,1,0:T(8,128)(2,1)S(1)}) custom-call(s32[3,128]{1,0:T(4,128)S(1)} %pad_add_fusion.dmeta, bf16[16,3,8,64,128]{4,3,2,1,0:T(8,128)(2,1)} %bitcast.63, bf16[128,32,128]{2,1,0:T(8,128)(2,1)S(1)} %broadcast_select_fusion.down), custom_call_target="tpu_custom_call" | custom-call | flops 134217728 | bytes 8388608 | tf_op jit(solution)/shard_map/down_kernel/pallas_call | solution.py:228
  69.8 1.3 copy-done.1
  71.1 0.8 copy-done.3
  71.9 0.0 all-to-all-done.2
  71.9 1.0 copy-done.4
  72.9 11.5 %layer_kernel.1 = (bf16[16,24,32,128]{3,2,1,0:T(8,128)(2,1)}, bf16[14,64,128]{2,1,0:T(8,128)(2,1)S(1)}, bf16[28,64,128]{2,1,0:T(8,128)(2,1)S(1)}) custom-call(s32[16,32]{1,0:T(8,128)S(1)} %copy.99.meta, s32[3,128]{1,0:T(4,128)S(1)} %pad_add_fusion.dmeta, bf16[16,3,8,64,128]{4,3,2,1,0:T(8,128)(2,1)} %bitcast.64, bf16[16,16,32,128]{3,2,1,0:T(8,128)(2,1)S(1)} %bitcast.61, ...), custom_call_target="tpu_custom_call" | custom-call | flops 536870912 | bytes 8388608 | tf_op jit(solution)/shard_map/layer_kernel/pallas_call | solution.py:249
  84.4 6.4 %output_kernel.1 = bf16[16,2,8,64,128]{4,3,2,1,0:T(8,128)(2,1)} custom-call(s32[16,32]{1,0:T(8,128)S(1)} %copy.99.meta, s32[3,128]{1,0:T(4,128)S(1)} %pad_add_fusion.dmeta, bf16[16,16,32,128]{3,2,1,0:T(8,128)(2,1)S(1)} %bitcast.62, bf16[128,64,64]{2,1,0:T(8,128)(2,1)S(1)} %copy-done.2, bf16[14,64,128]{2,1,0:T(8,128)(2,1)S(1)} %get-tuple-element.22.hidden_split, ...), custom_call_target="tpu_custom_call" | custom-call | flops 268435456 | bytes 8388608 | tf_op jit(solution)/shard_map/output_kernel/pallas_call | solution.py:275
  90.7 0.0 reduce-scatter.2.cloned.1.call-update
  90.8 25.5 %all_to_all.42 = bf16[4,4,24,32,128]{4,3,2,1,0:T(8,128)(2,1)S(1)} all-to-all(bf16[4,4,24,32,128]{4,3,2,1,0:T(8,128)(2,1)} %bitcast.68), channel_id=1, replica_groups={{0,64,128,192},{16,80,144,208},{32,96,160,224},{48,112,176,240},{1,17,3..., dimensions={0} | all-to-all | bytes 6291456 | tf_op jit(solution)/shard_map/all_to_all | solution.py:315
  116.2 1.6 reduce_sum.24
  117.8 12.3 %all_to_all.43 = bf16[4,24,32,128]{3,2,1,0:T(8,128)(2,1)S(1)} all-to-all(bf16[4,24,32,128]{3,2,1,0:T(8,128)(2,1)} %reduce_sum.24), channel_id=1, replica_groups={{0,16,32,48},{64,80,96,112},{128,144,160,176},{192,208,224,240},{1,65,1..., dimensions={0} | all-to-all | bytes 1572864 | tf_op jit(solution)/shard_map/all_to_all | solution.py:315
  130.1 0.1 reduce_sum.25
  130.3 0.7 slice.70
  131.0 7.4 %all-to-all-start.5 = ((bf16[16,32,128]{2,1,0:T(8,128)(2,1)}), bf16[16,32,128]{2,1,0:T(8,128)(2,1)S(1)}, u32[]{:S(2)}, u32[]{:S(2)}) async-start(bf16[16,32,128]{2,1,0:T(8,128)(2,1)} %slice.70), calls=%async_computation.6 | async-start | bytes 262144 | tf_op jit(solution)/shard_map/all_to_all | solution.py:432
  138.3 8.6 %all-to-all-done.5 = bf16[16,32,128]{2,1,0:T(8,128)(2,1)S(1)} async-done(((bf16[16,32,128]{2,1,0:T(8,128)(2,1)}), bf16[16,32,128]{2,1,0:T(8,128)(2,1)S(1)}, u32[]{:S(2)}, u32[]{:S(2)}) %all-to-all-start.5) | async-done | bytes 131104 | tf_op jit(solution)/shard_map/all_to_all | solution.py:432
  146.9 0.1 broadcast_select_fusion.1
  147.0 0.1 broadcast_in_dim.75
  147.1 11.9 %all_to_all.44 = bf16[4,24,32,128]{3,2,1,0:T(8,128)(2,1)S(1)} all-to-all(bf16[4,24,32,128]{3,2,1,0:T(8,128)(2,1)S(1)} %broadcast_in_dim.75), channel_id=1, replica_groups={{0,16,32,48},{64,80,96,112},{128,144,160,176},{192,208,224,240},{1,65,1..., dimensions={0} | all-to-all | bytes 1572864 | tf_op jit(solution)/shard_map/all_to_all | solution.py:315
  159.0 0.6 broadcast_in_dim.76
  159.6 23.8 %all_to_all.45 = bf16[4,4,24,32,128]{4,3,2,1,0:T(8,128)(2,1)S(1)} all-to-all(bf16[4,4,24,32,128]{4,3,2,1,0:T(8,128)(2,1)S(1)} %broadcast_in_dim.76), channel_id=1, replica_groups={{0,64,128,192},{16,80,144,208},{32,96,160,224},{48,112,176,240},{1,17,3..., dimensions={0} | all-to-all | bytes 6291456 | tf_op jit(solution)/shard_map/all_to_all | solution.py:315
  183.4 1.1 slice.74
  184.5 0.5 slice_bitcast_fusion
  185.0 1.1 copy.101
  186.0 1.1 copy.100
  187.1 2.0 convolution_convert_fusion
  189.1 1.8 convolution_convert_fusion.1
  (29 shorter events, 0.2 us)
Async XLA Ops:
  7.2 0.9 copy-start
  7.2 56.2 %all-gather.3.cloned.1.call-start = ((), (), s32[]{:S(2)}) async-start(), calls=%async_computation.10 | async-start | bytes 6684672 | tf_op jit(solution)/shard_map/all_gather | solution.py:368
  46.9 6.0 %copy-start.6 = (s32[16]{0:T(128)S(1)}, s32[16]{0:T(128)}, u32[]{:S(2)}) copy-start(s32[16]{0:T(128)} %param.20) | copy-start | bytes 196
  46.9 6.2 %copy-start.5 = (s32[128,2]{0,1:T(2,128)S(1)}, s32[128,2]{0,1:T(2,128)}, u32[]{:S(2)}) copy-start(s32[128,2]{0,1:T(2,128)} %param.19) | copy-start | bytes 3076
  48.6 23.2 %all-to-all-start.2 = ((bf16[4,4,16,32,128]{4,3,2,1,0:T(8,128)(2,1)}), bf16[4,4,16,32,128]{4,3,2,1,0:T(8,128)(2,1)S(1)}, u32[]{:S(2)}, u32[]{:S(2)}) async-start(bf16[4,4,16,32,128]{4,3,2,1,0:T(8,128)(2,1)} %broadcast_in_dim.72), calls=%async_computation.2 | async-start | bytes 4194304 | tf_op jit(solution)/shard_map/all_to_all | solution.py:315
  52.7 134.5 %reduce-scatter.2.cloned.1.call-start = ((), (), s32[]{:S(2)}) async-start(), calls=%async_computation.9 | async-start | bytes 4456448 | tf_op jit(solution)/shard_map/reduce_scatter | solution.py:421
  69.8 1.3 copy-start.1
  71.1 0.8 copy-start.3
  71.9 1.0 copy-start.4
  72.9 11.5 %copy-start.2 = (bf16[128,64,64]{2,1,0:T(8,128)(2,1)S(1)}, bf16[128,64,64]{2,1,0:T(8,128)(2,1)}, u32[]{:S(2)}) copy-start(bf16[128,64,64]{2,1,0:T(8,128)(2,1)} %copy-done.1) | copy-start | bytes 3145732
  131.0 15.9 %all-to-all-start.5 = ((bf16[16,32,128]{2,1,0:T(8,128)(2,1)}), bf16[16,32,128]{2,1,0:T(8,128)(2,1)S(1)}, u32[]{:S(2)}, u32[]{:S(2)}) async-start(bf16[16,32,128]{2,1,0:T(8,128)(2,1)} %slice.70), calls=%async_computation.6 | async-start | bytes 262144 | tf_op jit(solution)/shard_map/all_to_all | solution.py:432
Sparse Core Ops, SparseCore 0:
  10.7 52.6 all-gather.2
  90.9 61.1 reduce-scatter.1

commit v2 on v1

v2 whole, which is shorter than its diff:
```python
import jax
import jax.numpy as jnp
from jax import lax
from jax.experimental import pallas as pl
from jax.experimental.pallas import tpu as pltpu
from jax.sharding import PartitionSpec as P

FF = 14336
TILE = 64
HALF = TILE // 2
DEPTH = 8
D_OWN = 8
F_OWN = 14
GROUPS = 16
SIDE = 4
CHUNKS = 4
BF = jnp.bfloat16
F32 = jnp.float32


def tn(a, b):
    return lax.dot_general(a, b, (((0,), (0,)), ((), ())), preferred_element_type=F32)


def nn(a, b):
    return lax.dot_general(a, b, (((1,), (0,)), ((), ())), preferred_element_type=F32)


def nt(a, b):
    return lax.dot_general(a, b, (((1,), (1,)), ((), ())), preferred_element_type=F32)


def unpack(tile):
    return jnp.concatenate([tile[:, :TILE], tile[:, TILE:]], axis=0)


def pack(values):
    return jnp.concatenate([values[:HALF], values[HALF:]], axis=1)


def turn_kernel(down, down_t, turned, sems):
    span = GROUPS * DEPTH // CHUNKS
    for n in range(CHUNKS):
        flat = pl.ds(n * span, span)

        @pl.loop(n * span, (n + 1) * span, step=2 * DEPTH)
        def _(base):
            for c in range(2 * DEPTH):
                turned[base + c] = unpack(down[base + c]).T

        pltpu.make_async_copy(turned.at[flat], down_t.at[flat], sems.at[n]).start()
    for n in range(CHUNKS):
        flat = pl.ds(n * span, span)
        pltpu.make_async_copy(turned.at[flat], down_t.at[flat], sems.at[n]).wait()


def pieces(place):
    first = [(place[0] + SIDE - k) & (SIDE - 1) for k in range(SIDE)]
    second = [(place[1] + SIDE - k) & (SIDE - 1) for k in range(SIDE)]
    return [SIDE * i + j for i in first for j in second]


def tile_loads(gu, tiles, sems, n):
    rows = pl.ds(n * (GROUPS // CHUNKS), GROUPS // CHUNKS)
    return [
        pltpu.make_async_copy(
            gu[k].at[:, rows], tiles.at[pl.ds(k * SIDE, SIDE), rows], sems.at[k, n]
        )
        for k in range(SIDE)
    ]


def layer_kernel(
    place,
    meta,
    dmeta,
    act,
    down,
    gu_0,
    gu_1,
    gu_2,
    gu_3,
    grads_0,
    grads_1,
    grads_2,
    grads_3,
    hidden_split,
    pre,
    pairs,
    tiles,
    tokens,
    cot,
    grads_v,
    acc,
    acc_dh,
    strided,
    tile_sems,
    sems,
):
    span = GROUPS // CHUNKS
    gu = (gu_0, gu_1, gu_2, gu_3)
    grads = (grads_0, grads_1, grads_2, grads_3)
    slot = pieces(place)

    def plane(n, which, target):
        rows = pl.ds(n * span, span)
        return pltpu.make_async_copy(act.at[rows, which], target.at[rows], sems.at[which, n])

    load_cot = [plane(n, 1, cot) for n in range(CHUNKS)]
    load_pairs = [plane(n, 2, pairs) for n in range(CHUNKS)]
    load_tiles = [tile_loads(gu, tiles, tile_sems, n) for n in range(CHUNKS)]
    load_tokens = pltpu.make_async_copy(act.at[:, 0], tokens, sems.at[0, 0])
    for copy in load_cot:
        copy.start()
    for n in range(CHUNKS):
        load_pairs[n].start()
        for copy in load_tiles[n]:
            copy.start()
    load_tokens.start()
    for f in range(F_OWN):
        acc_dh[f] = jnp.zeros((TILE, 128), F32)
        acc[f] = jnp.zeros((128, TILE), F32)
        acc[F_OWN + f] = jnp.zeros((128, TILE), F32)

    for n in range(CHUNKS):
        load_cot[n].wait()

        @pl.loop(n * span, (n + 1) * span, unroll=span)
        def _(e):
            parts = [
                nn(unpack(down[e * DEPTH + c]), cot[e, dmeta[1, e * DEPTH + c]])
                for c in range(DEPTH)
            ]
            for c in range(DEPTH):
                acc_dh[dmeta[0, e * DEPTH + c]] += parts[c]

    for n in range(CHUNKS):
        load_pairs[n].wait()
        for copy in load_tiles[n]:
            copy.wait()

        @pl.loop(n * span, (n + 1) * span, unroll=span)
        def _(q):
            for base in range(0, 2 * DEPTH, 4):
                parts = []
                for m in range(base, base + 4):
                    tile = unpack(tiles[m, q])
                    row = meta[q, slot[m]]
                    odd = jnp.broadcast_to(row % 2, tile.shape) > 0
                    none = jnp.zeros_like(tile)
                    tall = jnp.concatenate(
                        [jnp.where(odd, none, tile), jnp.where(odd, tile, none)], axis=0
                    )
                    pair = 2 * (row // 2)
                    both = jnp.concatenate([pairs[q, pair], pairs[q, pair + 1]], axis=0)
                    parts.append(nn(both, tall))
                for m in range(base, base + 4):
                    acc[meta[q, 2 * DEPTH + slot[m]]] += parts[m - base]

    for f in range(F_OWN):
        strided[f, pl.ds(0, HALF, stride=2), :] = acc_dh[f, :HALF]
        strided[f, pl.ds(1, HALF, stride=2), :] = acc_dh[f, HALF:]
    for f in range(F_OWN):
        back = strided[f]
        gate = acc[f].T
        up = acc[F_OWN + f].T
        sig = jax.nn.sigmoid(gate)
        activated = gate * sig
        pre[f] = (back * up * (sig * (1.0 + gate * (1.0 - sig)))).astype(BF)
        pre[F_OWN + f] = (back * activated).astype(BF)
        acc_dh[f] = activated * up
    for f in range(F_OWN):
        hidden_split[f, :HALF] = acc_dh[f, pl.ds(0, HALF, stride=2), :].astype(BF)
        hidden_split[f, HALF:] = acc_dh[f, pl.ds(1, HALF, stride=2), :].astype(BF)

    @pl.loop(0, GROUPS, unroll=8)
    def _(q):
        for c in range(DEPTH):
            k = q * DEPTH + c
            got = nt(hidden_split[dmeta[0, k]], cot[q, dmeta[1, k]])
            live = jnp.broadcast_to(dmeta[2, k], got.shape) > 0
            grads_v[q, GROUPS + c] = pack(jnp.where(live, got, 0.0).astype(BF))

    def stores(k, part, which):
        rows = pl.ds(SIDE * ((place[0] + k) & (SIDE - 1)), SIDE)
        return pltpu.make_async_copy(
            grads_v.at[rows, part], grads[k].at[:, part], sems.at[3 + which, k]
        )

    in_gu, in_down = pl.ds(0, GROUPS), pl.ds(GROUPS, DEPTH)
    for k in range(SIDE):
        stores(k, in_down, 0).start()
    load_tokens.wait()

    @pl.loop(0, GROUPS, unroll=8)
    def _(q):
        for m in range(2 * DEPTH):
            got = nt(tokens[q, meta[q, m]], pre[meta[q, 2 * DEPTH + m]])
            grads_v[m, q] = pack(got.astype(BF))

    for k in range(SIDE):
        stores(k, in_gu, 1).start()
    for k in range(SIDE):
        stores(k, in_down, 0).wait()
        stores(k, in_gu, 1).wait()


def output_kernel(
    place,
    meta,
    dmeta,
    down_t,
    hidden_split,
    pre,
    gu_0,
    gu_1,
    gu_2,
    gu_3,
    partials,
    tiles,
    turned,
    sums,
    acc,
    tile_sems,
    sems,
):
    span = GROUPS // CHUNKS
    slot = pieces(place)
    zero_block = jnp.zeros((TILE, 128), F32)

    def load_turned(n):
        flat = pl.ds(n * span * DEPTH, span * DEPTH)
        return pltpu.make_async_copy(down_t.at[flat], turned.at[flat], sems.at[0, n])

    def store(n):
        rows = pl.ds(n * span, span)
        return pltpu.make_async_copy(sums.at[rows], partials.at[rows], sems.at[1, n])

    load_tiles = [tile_loads((gu_0, gu_1, gu_2, gu_3), tiles, tile_sems, n) for n in range(CHUNKS)]
    for n in range(CHUNKS):
        load_turned(n).start()
        for copy in load_tiles[n]:
            copy.start()

    for n in range(CHUNKS):
        load_turned(n).wait()
        for copy in load_tiles[n]:
            copy.wait()

        @pl.loop(n * span, (n + 1) * span, unroll=span)
        def _(q):
            for r in range(D_OWN):
                acc[0, r] = zero_block
                acc[1, r] = zero_block
            for base in range(0, DEPTH, 4):
                parts = []
                for c in range(base, base + 4):
                    k = q * DEPTH + c
                    parts.append(nn(turned[k], hidden_split[dmeta[0, k]]))
                for c in range(base, base + 4):
                    acc[0, dmeta[1, q * DEPTH + c]] += parts[c - base]
            for base in range(0, 2 * DEPTH, 4):
                parts = []
                for m in range(base, base + 4):
                    parts.append(nn(unpack(tiles[m, q]), pre[meta[q, 2 * DEPTH + slot[m]]]))
                for m in range(base, base + 4):
                    acc[1, meta[q, slot[m]]] += parts[m - base]
            for r in range(D_OWN):
                sums[q, 0, r] = acc[0, r].astype(BF)
                sums[q, 1, r] = acc[1, r].astype(BF)

        store(n).start()
    for n in range(CHUNKS):
        store(n).wait()


def turn_back(summed, layer_output, grad_tokens, ordered):
    width = D_OWN * TILE
    for r in range(D_OWN):
        for odd in range(2):
            rows = summed[pl.ds(width + r * TILE + odd * HALF, HALF), :]
            ordered[pl.ds(r * TILE + odd, HALF, stride=2), :] = rows.astype(F32)
    for n in range(width // 128):
        lanes = pl.ds(n * 128, 128)
        layer_output[:, lanes] = summed[lanes, :].T
        grad_tokens[:, lanes] = ordered[lanes, :].T.astype(BF)


def finish_kernel(
    place,
    summed,
    full_0,
    full_1,
    full_2,
    full_3,
    layer_output,
    grad_tokens,
    gate,
    up,
    down,
    ordered,
    sems,
):
    full = (full_0, full_1, full_2, full_3)
    for phase in range(2):
        if phase == 1:
            turn_back(summed, layer_output, grad_tokens, ordered)
        for k in range(SIDE):
            first = (place[0] + SIDE - k) & (SIDE - 1)
            for j in range(SIDE):
                second = (place[1] + SIDE - j) & (SIDE - 1)
                slot = SIDE * k + j
                to_down = pltpu.make_async_copy(
                    full[k].at[j, pl.ds(GROUPS, DEPTH)], down.at[SIDE * first + second], sems.at[1, slot]
                )
                depth = SIDE * (first & 1) + second
                source = full[k].at[j, pl.ds(0, GROUPS)]
                to_gate = pltpu.make_async_copy(source, gate.at[:, depth], sems.at[0, slot])
                to_up = pltpu.make_async_copy(source, up.at[:, depth], sems.at[0, slot])
                for copy, when in ((to_gate, first < 2), (to_up, first >= 2)):

                    @pl.when(when)
                    def _(copy=copy):
                        if phase == 0:
                            copy.start()
                        else:
                            copy.wait()

                if phase == 0:
                    to_down.start()
                else:
                    to_down.wait()


SMEM = pl.BlockSpec(memory_space=pltpu.SMEM)
VMEM = pl.BlockSpec(memory_space=pltpu.VMEM)
ANY = pl.BlockSpec(memory_space=pl.ANY)
LIMIT = 48 * 1024 * 1024
SMALL = 16 * 1024 * 1024


def turn(down):
    whole = (GROUPS * DEPTH, TILE, TILE)
    return pl.pallas_call(
        turn_kernel,
        out_shape=jax.ShapeDtypeStruct(whole, BF),
        in_specs=[VMEM],
        out_specs=ANY,
        scratch_shapes=[pltpu.VMEM(whole, BF), pltpu.SemaphoreType.DMA((CHUNKS,))],
        compiler_params=pltpu.CompilerParams(vmem_limit_bytes=LIMIT),
        cost_estimate=pl.CostEstimate(flops=2**26, bytes_accessed=2**22, transcendentals=0),
        name="turn_kernel",
    )(down)


def layer(place, meta, dmeta, act, down, gu):
    block = (GROUPS, D_OWN, TILE, 128)
    piece = jax.ShapeDtypeStruct((SIDE, 3 * DEPTH, HALF, 128), BF)
    *grads, hidden_split, pre = pl.pallas_call(
        layer_kernel,
        out_shape=(piece,) * SIDE
        + (
            jax.ShapeDtypeStruct((F_OWN, TILE, 128), BF),
            jax.ShapeDtypeStruct((2 * F_OWN, TILE, 128), BF),
        ),
        in_specs=[SMEM, SMEM, SMEM, ANY, VMEM] + [ANY] * SIDE,
        out_specs=(ANY,) * SIDE + (VMEM, VMEM),
        scratch_shapes=[
            pltpu.VMEM(block, BF),
            pltpu.VMEM((2 * DEPTH, GROUPS, HALF, 128), BF),
            pltpu.VMEM(block, BF),
            pltpu.VMEM(block, BF),
            pltpu.VMEM((GROUPS, 3 * DEPTH, HALF, 128), BF),
            pltpu.VMEM((2 * F_OWN, 128, TILE), F32),
            pltpu.VMEM((F_OWN, TILE, 128), F32),
            pltpu.VMEM((F_OWN, TILE, 128), F32),
            pltpu.SemaphoreType.DMA((SIDE, CHUNKS)),
            pltpu.SemaphoreType.DMA((5, CHUNKS)),
        ],
        compiler_params=pltpu.CompilerParams(vmem_limit_bytes=LIMIT),
        cost_estimate=pl.CostEstimate(flops=2**29, bytes_accessed=2**23, transcendentals=0),
        name="layer_kernel",
    )(place, meta, dmeta, act, down, *gu)
    return grads, hidden_split, pre


def output_part(place, meta, dmeta, down_t, hidden_split, pre, gu):
    return pl.pallas_call(
        output_kernel,
        out_shape=jax.ShapeDtypeStruct((GROUPS, 2, D_OWN, TILE, 128), BF),
        in_specs=[SMEM, SMEM, SMEM, ANY, VMEM, VMEM] + [ANY] * SIDE,
        out_specs=ANY,
        scratch_shapes=[
            pltpu.VMEM((2 * DEPTH, GROUPS, HALF, 128), BF),
            pltpu.VMEM((GROUPS * DEPTH, TILE, TILE), BF),
            pltpu.VMEM((GROUPS, 2, D_OWN, TILE, 128), BF),
            pltpu.VMEM((2, D_OWN, TILE, 128), F32),
            pltpu.SemaphoreType.DMA((SIDE, CHUNKS)),
            pltpu.SemaphoreType.DMA((2, CHUNKS)),
        ],
        compiler_params=pltpu.CompilerParams(vmem_limit_bytes=LIMIT),
        cost_estimate=pl.CostEstimate(flops=2**28, bytes_accessed=2**23, transcendentals=0),
        name="output_kernel",
    )(place, meta, dmeta, down_t, hidden_split, pre, *gu)


def finish(place, summed, full):
    tiles = jax.ShapeDtypeStruct((GROUPS, DEPTH, HALF, 128), BF)
    width = D_OWN * TILE
    rows = jax.ShapeDtypeStruct((128, width), BF)
    return pl.pallas_call(
        finish_kernel,
        out_shape=(rows,) * 2 + (tiles,) * 3,
        in_specs=[SMEM, VMEM] + [ANY] * SIDE,
        out_specs=(VMEM,) * 2 + (ANY,) * 3,
        scratch_shapes=[pltpu.VMEM((width, 128), F32), pltpu.SemaphoreType.DMA((2, SIDE * SIDE))],
        compiler_params=pltpu.CompilerParams(vmem_limit_bytes=SMALL),
        cost_estimate=pl.CostEstimate(flops=0, bytes_accessed=2**22, transcendentals=0),
        name="finish_kernel",
    )(place, summed, *full)


def split_order(size):
    n = jnp.arange(size, dtype=jnp.int32)
    block, inner = n // TILE, n % TILE
    source = block * TILE + 2 * (inner % HALF) + inner // HALF
    return (source[:, None] == n[None, :]).astype(BF)


def lines(second):
    groups = []
    for mp in range(GROUPS):
        for other in range(SIDE):
            along_x = (mp % 2 == 0) != second
            groups.append(
                [
                    ((n * SIDE + other) if along_x else (other * SIDE + n)) * GROUPS + mp
                    for n in range(SIDE)
                ]
            )
    return groups


def shift(value, second, count):
    pairs = [
        (line[n], line[(n + count) % SIDE]) for line in lines(second) for n in range(SIDE)
    ]
    return lax.ppermute(value, ("dp", "mp"), pairs)


def to_replicas(piece):
    row = jnp.stack([piece] + [shift(piece, True, k) for k in range(1, SIDE)])
    return [row] + [shift(row, False, k) for k in range(1, SIDE)]


def from_replicas(parts, second):
    got = parts
    rows = sum(part.astype(F32) for part in got).astype(BF)
    ahead = [
        lax.dynamic_index_in_dim(rows, (second + k) % SIDE, 0, keepdims=False)
        for k in range(SIDE)
    ]
    got = [ahead[0]] + [shift(ahead[k], True, k) for k in range(1, SIDE)]
    return sum(part.astype(F32) for part in got).astype(BF)


def per_device(
    tokens,
    gate_tiles,
    gate_index,
    gate_count,
    up_tiles,
    up_index,
    up_count,
    down_tiles,
    down_index,
    down_count,
    grad_output,
):
    me = lax.axis_index("mp")
    replica = lax.axis_index("dp")
    crossed = me % 2
    turned = (replica % SIDE) * SIDE + replica // SIDE
    part = jnp.where(crossed == 1, turned, replica)
    place = jnp.stack([part // SIDE, part % SIDE]).astype(jnp.int32)
    width = tokens.shape[1]
    order = split_order(width)
    eye = jnp.eye(width, dtype=BF)
    groups = jnp.arange(GROUPS, dtype=jnp.int32)[:, None]
    slots = jnp.arange(DEPTH, dtype=jnp.int32)[None, :]

    tokens_t = jnp.einsum("pi,ti->pt", order, tokens, preferred_element_type=F32).astype(BF)
    grad_t = jnp.einsum("pi,ti->pt", eye, grad_output, preferred_element_type=F32).astype(BF)
    tokens_p = jnp.einsum("ti,pi->tp", tokens, order, preferred_element_type=F32).astype(BF)
    tokens_p = tokens_p.reshape(128, width // 128, 128).transpose(1, 0, 2).reshape(width, 128)
    own = jnp.concatenate([tokens_t, grad_t, tokens_p], axis=0)
    own, gate_index, up_index, gate_tiles, up_tiles = lax.optimization_barrier(
        (own, gate_index, up_index, gate_tiles, up_tiles)
    )
    act = lax.all_gather(own, "mp", axis=0)
    act = act.reshape(GROUPS, 3, D_OWN, TILE, 128)

    def blocks(index):
        return index.reshape(GROUPS, DEPTH, 2)

    is_up = part // DEPTH
    depth = part % DEPTH
    gate_t = lax.dynamic_index_in_dim(
        gate_tiles.reshape(GROUPS, DEPTH, HALF, 128), depth, 1, keepdims=False
    )
    up_t = lax.dynamic_index_in_dim(
        up_tiles.reshape(GROUPS, DEPTH, HALF, 128), depth, 1, keepdims=False
    )
    count = jnp.where(is_up == 1, up_count, gate_count)
    my_live = (depth < count)[:, None, None]
    mine = jnp.where(my_live, jnp.where(is_up == 1, up_t, gate_t), 0)
    gate_b, up_b = blocks(gate_index), blocks(up_index)
    notes = jnp.concatenate(
        [
            gate_b[..., 0] - me * D_OWN,
            up_b[..., 0] - me * D_OWN,
            gate_b[..., 1] - groups * F_OWN,
            up_b[..., 1] - groups * F_OWN + F_OWN,
        ],
        axis=1,
    ).astype(BF)
    notes = jnp.pad(notes[:, None, :], ((0, 0), (0, 7), (0, 128 - 4 * DEPTH)))
    sent = lax.all_to_all(
        jnp.concatenate([mine, notes], axis=1), "mp", 0, 0, tiled=True
    )
    meta = sent[:, HALF, : 4 * DEPTH].astype(jnp.int32).reshape(GROUPS, 2, SIDE, SIDE)
    same = (groups % 2 == crossed)[..., None, None]
    meta = jnp.where(same, meta, meta.swapaxes(2, 3)).reshape(GROUPS, 4 * DEPTH)
    gu = to_replicas(sent[:, :HALF])

    down_b = blocks(down_index)
    down_live = slots < down_count[:, None]
    dmeta = jnp.stack(
        [
            (down_b[..., 0] - me * F_OWN).reshape(-1),
            (down_b[..., 1] - groups * D_OWN).reshape(-1),
            down_live.astype(jnp.int32).reshape(-1),
        ]
    )
    down = jnp.where(
        down_live.reshape(-1)[:, None, None], down_tiles.reshape(GROUPS * DEPTH, HALF, 128), 0
    )

    down_t = turn(down)
    down, down_t = lax.optimization_barrier((down, down_t))
    grads, hidden_split, pre = layer(place, meta, dmeta, act, down, gu)
    grads = [grads[0]] + [shift(grads[k], False, k) for k in range(1, SIDE)]
    partials = output_part(place, meta, dmeta, down_t, hidden_split, pre, gu)
    *grads, partials = lax.optimization_barrier((*grads, partials))

    summed = lax.psum_scatter(
        partials.reshape(GROUPS * 2 * width, 128), "mp", scatter_dimension=0, tiled=True
    )

    got = from_replicas(grads, part % SIDE)
    back = lax.all_to_all(got[:GROUPS], "mp", 0, 0, tiled=True)
    piece = jnp.concatenate([jnp.where(my_live, back, 0), got[GROUPS:]], axis=0)
    flat = (GROUPS * DEPTH * HALF, 128)
    layer_output, grad_tokens, *tile_grads = finish(place, summed, to_replicas(piece))
    grad_gate, grad_up, grad_down = (g.reshape(flat) for g in tile_grads)
    return (layer_output, grad_tokens, grad_gate, grad_up, grad_down)


def solution(mesh):
    return jax.shard_map(
        per_device,
        mesh=mesh,
        in_specs=(
            P("dp", "mp"),
            P("mp", None),
            P("mp", None),
            P("mp"),
            P("mp", None),
            P("mp", None),
            P("mp"),
            P("mp", None),
            P("mp", None),
            P("mp"),
            P("dp", "mp"),
        ),
        out_specs=(P("dp", "mp"), P("dp", "mp"), P("mp", None), P("mp", None), P("mp", None)),
        check_vma=False,
    )
```

time: 198 us -> 173 us (0.87); the launches traced: 198 us -> 170 us
  blocking collectives: 105 us -> 0 us
  waiting for transfers between devices: 16.9 us -> 69.5 us
  starting transfers between devices: 11.4 us -> 44.4 us
  local copies, waits for them, and re-layouts: 14 us -> 7.57 us
  matrix products: 5.36 us -> 1.66 us
  Pallas kernels: 24.2 us -> 26.3 us
    all_to_all x6 -> x0, blocking collectives: 105 us -> none  [the longest x5 84.5 us: exchange(): lax.all_to_all(parts, ('dp', 'mp'), 0, 0, tiled=True, axis_index_groups=l...]
    ppermute x0 -> x18, waiting for transfers between devices: none -> 48.6 us  [shift(): return lax.ppermute(value, ('dp', 'mp'), pairs)]
    ppermute x0 -> x18, starting transfers between devices: none -> 26.9 us  [shift(): return lax.ppermute(value, ('dp', 'mp'), pairs)]
    all_to_all x1, waiting for transfers between devices: 0.01 us -> 9.85 us  [per_device(): lax.all_to_all(jnp.concatenate([mine, notes], axis=1), 'mp', 0, 0, tiled=...]
    all_gather x1, waiting for transfers between devices: 8.33 us -> 1.14 us  [per_device(): act = lax.all_gather(own, 'mp', axis=0)]
    all_to_all x1, starting transfers between devices: 4.03 us -> 9.98 us  [per_device(): lax.all_to_all(jnp.concatenate([mine, notes], axis=1), 'mp', 0, 0, tiled=...]
    dot_general x2 -> x0, matrix products: 3.79 us -> none  [the longest x1 1.98 us: per_device(): jnp.einsum('pt,pi->ti', summed[width:], order, preferred_element_type=F32)]
    transpose x3 -> x0, local copies, waits for them, and re-layouts: 2.62 us -> none  [the longest x2 1.54 us: per_device(): grad_up = full[DEPTH:, :GROUPS].transpose(1, 0, 2, 3).reshape(flat)]
  transfers between devices with their start and end apart: 4 -> 22, of which waited for: 2 -> 14; matrix products, arithmetic and copies ran while one was open for 8% -> 5% of each run, Pallas kernels for 3% -> 6%
where the time goes in v2:
time: 173 us; the launch traced here: 170 us
  waiting for transfers between devices  69.5 us (40%)
  starting transfers between devices  44.4 us (26%)
  Pallas kernels  26.3 us (15%)
  between operations  14.6 us (8%)
  local copies, waits for them, and re-layouts  7.57 us (4%)
  other arithmetic  6.11 us (4%)
    ppermute x18, waiting for transfers between devices, shift(): return lax.ppermute(value, ('dp', 'mp'), pairs)  48.6 us
    ppermute x18, starting transfers between devices, shift(): return lax.ppermute(value, ('dp', 'mp'), pairs)  26.9 us
    pallas_call x1, Pallas kernels, layer(): pl.pallas_call(layer_kernel, out_shape=(piece,) * SIDE + (jax.ShapeDtypeS...  12.4 us
    all_to_all x1, starting transfers between devices, per_device(): lax.all_to_all(jnp.concatenate([mine, notes], axis=1), 'mp', 0, 0, tiled=...  9.98 us
    all_to_all x1, waiting for transfers between devices, per_device(): back = lax.all_to_all(got[:GROUPS], 'mp', 0, 0, tiled=True)  9.85 us
    all_to_all x1, waiting for transfers between devices, per_device(): lax.all_to_all(jnp.concatenate([mine, notes], axis=1), 'mp', 0, 0, tiled=...  9.85 us
    all_to_all x1, starting transfers between devices, per_device(): back = lax.all_to_all(got[:GROUPS], 'mp', 0, 0, tiled=True)  7.44 us
    pallas_call x1, Pallas kernels, output_part(): pl.pallas_call(output_kernel, out_shape=jax.ShapeDtypeStruct((GROUPS, 2,...  7.42 us
  transfers between devices with their start and end apart: 22, of which 14 were waited for; matrix products, arithmetic and copies ran while one was open for 5% of the time, Pallas kernels for 6%

profile of v2, /device:TPU:1, one launch (start us, length us, event | category | flops | bytes accessed | tf_op | source)
XLA Modules:
  0.0 170.2 jit_solution(12099211596346826004)
XLA Ops:
  7.3 0.8 copy-done
  8.1 0.4 convolution_convert_fusion.1
  8.4 0.1 copy.37
  8.6 1.3 convolution_convert_fusion
  9.9 0.8 pad_maximum_fusion.2
  11.1 0.1 copy.44
  11.5 0.1 copy.46
  11.7 0.1 fusion.14
  11.8 1.1 fusion.5
  12.9 0.7 pad_maximum_fusion.4
  13.6 10.0 %all-to-all-start = ((bf16[16,40,128]{2,1,0:T(8,128)(2,1)}), bf16[16,40,128]{2,1,0:T(8,128)(2,1)S(1)}, u32[]{:S(2)}, u32[]{:S(2)}) async-start(bf16[16,40,128]{2,1,0:T(8,128)(2,1)} %pad_maximum_fusion.4), calls=%async_computation | async-start | bytes 327680 | tf_op jit(solution)/shard_map/all_to_all | solution.py:528
  23.8 0.1 lt.117
  23.9 0.2 broadcast_select_fusion.down
  24.1 9.8 %all-to-all-done = bf16[16,40,128]{2,1,0:T(8,128)(2,1)S(1)} async-done(((bf16[16,40,128]{2,1,0:T(8,128)(2,1)}), bf16[16,40,128]{2,1,0:T(8,128)(2,1)S(1)}, u32[]{:S(2)}, u32[]{:S(2)}) %all-to-all-start) | async-done | bytes 163872 | tf_op jit(solution)/shard_map/all_to_all | solution.py:528
  34.0 0.7 slice_bitcast_fusion
  34.7 1.2 collective-permute-start
  35.9 2.5 %collective-permute-start.1 = (bf16[16,32,128]{2,1,0:T(8,128)(2,1)}, bf16[16,32,128]{2,1,0:T(8,128)(2,1)}, u32[]{:S(2)}, u32[]{:S(2)}) collective-permute-start(bf16[16,32,128]{2,1,0:T(8,128)(2,1)} %get-tuple-element.57), channel_id=1, source_target_pairs={{0,32},{16,48},{32,0},{48,16},{64,96},{80,112},{96,64},{112,80},{1... | collective-permute-start | bytes 393224 | tf_op jit(solution)/shard_map/ppermute | solution.py:448
  38.4 1.2 collective-permute-start.2
  39.7 0.1 sub.120
  39.8 0.1 sub.118
  39.9 0.1 reshape.322
  40.0 3.3 %turn_kernel.1.down_t = bf16[128,64,64]{2,1,0:T(8,128)(2,1)S(1)} custom-call(bf16[128,32,128]{2,1,0:T(8,128)(2,1)S(1)} %broadcast_select_fusion.down), custom_call_target="tpu_custom_call" | custom-call | flops 67108864 | bytes 4194304 | tf_op jit(solution)/shard_map/turn_kernel/pallas_call | solution.py:344
  43.4 1.2 pad_maximum_fusion.1.gu_0
  44.5 1.4 collective-permute-start.3
  45.9 2.8 %collective-permute-start.4 = (bf16[4,16,32,128]{3,2,1,0:T(8,128)(2,1)S(1)}, bf16[4,16,32,128]{3,2,1,0:T(8,128)(2,1)}, u32[]{:S(2)}, u32[]{:S(2)}) collective-permute-start(bf16[4,16,32,128]{3,2,1,0:T(8,128)(2,1)S(1)} %pad_maximum_fusion.1.gu_0), channel_id=1, source_target_pairs={{0,128},{64,192},{128,0},{192,64},{16,144},{80,208},{144,16},{208,... | collective-permute-start | bytes 1572872 | tf_op jit(solution)/shard_map/ppermute | solution.py:448
  48.7 1.0 collective-permute-start.5
  50.0 4.5 %collective-permute-done.3.gu_1 = bf16[4,16,32,128]{3,2,1,0:T(8,128)(2,1)S(1)} collective-permute-done((bf16[4,16,32,128]{3,2,1,0:T(8,128)(2,1)S(1)}, bf16[4,16,32,128]{3,2,1,0:T(8,128)(2,1)S(1)}, u32[]{:S(2)}, u32[]{:S(2)}) %collective-permute-start.3) | collective-permute-done | bytes 524320 | tf_op jit(solution)/shard_map/ppermute | solution.py:448
  54.5 6.8 %collective-permute-done.4.gu_2 = bf16[4,16,32,128]{3,2,1,0:T(8,128)(2,1)} collective-permute-done((bf16[4,16,32,128]{3,2,1,0:T(8,128)(2,1)S(1)}, bf16[4,16,32,128]{3,2,1,0:T(8,128)(2,1)}, u32[]{:S(2)}, u32[]{:S(2)}) %collective-permute-start.4) | collective-permute-done | bytes 524320 | tf_op jit(solution)/shard_map/ppermute | solution.py:448
  61.3 1.1 all-gather.3.cloned.1.call-done
  62.4 12.4 %layer_kernel.1 = (bf16[4,24,32,128]{3,2,1,0:T(8,128)(2,1)S(1)}, bf16[4,24,32,128]{3,2,1,0:T(8,128)(2,1)S(1)}, bf16[4,24,32,128]{3,2,1,0:T(8,128)(2,1)S(1)}, bf1...) custom-call(s32[2]{0:T(128)S(1)} %pad_add_fusion.1.place, ...), custom_call_target="tpu_custom_call" | custom-call | flops 536870912 | bytes 8388608 | tf_op jit(solution)/shard_map/layer_kernel/pallas_call | solution.py:359
  74.9 1.4 collective-permute-start.6
  76.2 2.7 %collective-permute-start.7 = (bf16[4,24,32,128]{3,2,1,0:T(8,128)(2,1)S(1)}, bf16[4,24,32,128]{3,2,1,0:T(8,128)(2,1)S(1)}, u32[]{:S(2)}, u32[]{:S(2)}) collective-permute-start(bf16[4,24,32,128]{3,2,1,0:T(8,128)(2,1)S(1)} %get-tuple-element.36), channel_id=1, source_target_pairs={{0,128},{64,192},{128,0},{192,64},{16,144},{80,208},{144,16},{208,... | collective-permute-start | bytes 2359304 | tf_op jit(solution)/shard_map/ppermute | solution.py:448
  78.9 1.0 collective-permute-start.8
  79.9 7.4 %output_kernel.1 = bf16[16,2,8,64,128]{4,3,2,1,0:T(8,128)(2,1)} custom-call(s32[2]{0:T(128)S(1)} %pad_add_fusion.1.place, s32[16,32]{1,0:T(8,128)S(1)} %copy.50.meta, s32[3,128]{1,0:T(4,128)S(1)} %pad_add_fusion.dmeta, bf16[128,64,64]{2,1,0:T(8,128)(2,1)S(1)} %turn_kernel.1.down_t, bf16[14,64,128]{2,1,0:T(8,128)(2,1)S(1)} %get-tuple-element.39.hidden_split, ...), custom_call_target="tpu_custom_call" | custom-call | flops 268435456 | bytes 8388608 | tf_op jit(solution)/shard_map/output_kernel/pallas_call | solution.py:388
  87.4 9.6 %collective-permute-done.7 = bf16[4,24,32,128]{3,2,1,0:T(8,128)(2,1)S(1)} collective-permute-done((bf16[4,24,32,128]{3,2,1,0:T(8,128)(2,1)S(1)}, bf16[4,24,32,128]{3,2,1,0:T(8,128)(2,1)S(1)}, u32[]{:S(2)}, u32[]{:S(2)}) %collective-permute-start.7) | collective-permute-done | bytes 786464 | tf_op jit(solution)/shard_map/ppermute | solution.py:448
  97.0 0.9 copy-done.8
  97.9 0.3 copy-done.10
  98.2 1.0 copy-done.3
  99.3 0.2 copy-done.7
  99.5 0.2 copy-done.9
  99.7 1.5 add_convert_fusion
  101.3 2.5 %collective-permute-start.10 = (bf16[24,32,128]{2,1,0:T(8,128)(2,1)S(1)}, bf16[24,32,128]{2,1,0:T(8,128)(2,1)S(1)}, u32[]{:S(2)}, u32[]{:S(2)}) collective-permute-start(bf16[24,32,128]{2,1,0:T(8,128)(2,1)S(1)} %get-tuple-element.53), channel_id=1, source_target_pairs={{0,32},{16,48},{32,0},{48,16},{64,96},{80,112},{96,64},{112,80},{1... | collective-permute-start | bytes 589832 | tf_op jit(solution)/shard_map/ppermute | solution.py:448
  103.9 0.9 collective-permute-start.11
  104.7 0.6 collective-permute-start.9
  105.3 2.4 %collective-permute-done.10 = bf16[24,32,128]{2,1,0:T(8,128)(2,1)S(1)} collective-permute-done((bf16[24,32,128]{2,1,0:T(8,128)(2,1)S(1)}, bf16[24,32,128]{2,1,0:T(8,128)(2,1)S(1)}, u32[]{:S(2)}, u32[]{:S(2)}) %collective-permute-start.10) | collective-permute-done | bytes 196640 | tf_op jit(solution)/shard_map/ppermute | solution.py:448
  107.8 1.8 %collective-permute-done.11 = bf16[24,32,128]{2,1,0:T(8,128)(2,1)S(1)} collective-permute-done((bf16[24,32,128]{2,1,0:T(8,128)(2,1)S(1)}, bf16[24,32,128]{2,1,0:T(8,128)(2,1)S(1)}, u32[]{:S(2)}, u32[]{:S(2)}) %collective-permute-start.11) | collective-permute-done | bytes 196640 | tf_op jit(solution)/shard_map/ppermute | solution.py:448
  109.6 0.9 collective-permute-done.9
  110.5 0.1 fusion.3
  110.6 0.7 slice.48
  111.3 7.4 %all-to-all-start.1 = ((bf16[16,32,128]{2,1,0:T(8,128)(2,1)}), bf16[16,32,128]{2,1,0:T(8,128)(2,1)S(1)}, u32[]{:S(2)}, u32[]{:S(2)}) async-start(bf16[16,32,128]{2,1,0:T(8,128)(2,1)} %slice.48), calls=%async_computation.2 | async-start | bytes 262144 | tf_op jit(solution)/shard_map/all_to_all | solution.py:561
  118.7 9.9 %all-to-all-done.1 = bf16[16,32,128]{2,1,0:T(8,128)(2,1)S(1)} async-done(((bf16[16,32,128]{2,1,0:T(8,128)(2,1)}), bf16[16,32,128]{2,1,0:T(8,128)(2,1)S(1)}, u32[]{:S(2)}, u32[]{:S(2)}) %all-to-all-start.1) | async-done | bytes 131104 | tf_op jit(solution)/shard_map/all_to_all | solution.py:561
  128.7 1.4 collective-permute-start.12
  130.1 1.8 %collective-permute-start.13 = (bf16[24,32,128]{2,1,0:T(8,128)(2,1)S(1)}, bf16[24,32,128]{2,1,0:T(8,128)(2,1)S(1)}, u32[]{:S(2)}, u32[]{:S(2)}) collective-permute-start(bf16[24,32,128]{2,1,0:T(8,128)(2,1)S(1)} %get-tuple-element.55), channel_id=1, source_target_pairs={{0,32},{16,48},{32,0},{48,16},{64,96},{80,112},{96,64},{112,80},{1... | collective-permute-start | bytes 589832 | tf_op jit(solution)/shard_map/ppermute | solution.py:448
  131.9 1.3 collective-permute-start.14
  133.2 1.6 collective-permute-done.12
  134.8 2.3 %collective-permute-done.13 = bf16[24,32,128]{2,1,0:T(8,128)(2,1)S(1)} collective-permute-done((bf16[24,32,128]{2,1,0:T(8,128)(2,1)S(1)}, bf16[24,32,128]{2,1,0:T(8,128)(2,1)S(1)}, u32[]{:S(2)}, u32[]{:S(2)}) %collective-permute-start.13) | collective-permute-done | bytes 196640 | tf_op jit(solution)/shard_map/ppermute | solution.py:448
  137.0 0.4 collective-permute-done.14
  137.5 0.1 pad_maximum_fusion.full_0
  137.7 2.2 %collective-permute-start.16 = (bf16[4,24,32,128]{3,2,1,0:T(8,128)(2,1)S(1)}, bf16[4,24,32,128]{3,2,1,0:T(8,128)(2,1)S(1)}, u32[]{:S(2)}, u32[]{:S(2)}) collective-permute-start(bf16[4,24,32,128]{3,2,1,0:T(8,128)(2,1)S(1)} %pad_maximum_fusion.full_0), channel_id=1, source_target_pairs={{0,128},{64,192},{128,0},{192,64},{16,144},{80,208},{144,16},{208,... | collective-permute-start | bytes 2359304 | tf_op jit(solution)/shard_map/ppermute | solution.py:448
  139.8 1.1 collective-permute-start.17
  140.9 17.5 %collective-permute-done.15.full_1 = bf16[4,24,32,128]{3,2,1,0:T(8,128)(2,1)S(1)} collective-permute-done((bf16[4,24,32,128]{3,2,1,0:T(8,128)(2,1)S(1)}, bf16[4,24,32,128]{3,2,1,0:T(8,128)(2,1)S(1)}, u32[]{:S(2)}, u32[]{:S(2)}) %collective-permute-start.15) | collective-permute-done | bytes 786464 | tf_op jit(solution)/shard_map/ppermute | solution.py:448
  158.4 0.7 collective-permute-done.17.full_3
  159.2 0.9 copy-done.4
  160.1 3.2 %finish_kernel.1 = (bf16[128,512]{1,0:T(8,128)(2,1)}, bf16[128,512]{1,0:T(8,128)(2,1)}, bf16[16,8,32,128]{3,2,1,0:T(8,128)(2,1)}, bf16[16,8,32,128]{3,2,1,0:T(8,128)(2,1)}, bf16[16,8,32,128]{3,2,1,0:T(8,128)(2,1)}) custom-call(s32[2]{0:T(128)S(1)} %pad_add_fusion.1.place, bf16[1024,128]{1,0:T(8,128)(2,1)S(1)} %copy-done.4, ...), custom_call_target="tpu_custom_call" | custom-call | bytes 4194304 | tf_op jit(solution)/shard_map/finish_kernel/pallas_call | solution.py:411
  (73 shorter events, 1.7 us)
Async XLA Ops:
  7.2 0.9 copy-start
  7.2 3.6 %copy-start.11 = (s32[128,2]{0,1:T(2,128)S(1)}, s32[128,2]{0,1:T(2,128)}, u32[]{:S(2)}) copy-start(s32[128,2]{0,1:T(2,128)} %param.13) | copy-start | bytes 3076
  7.2 3.8 %copy-start.12 = (s32[128,2]{0,1:T(2,128)S(1)}, s32[128,2]{0,1:T(2,128)}, u32[]{:S(2)}) copy-start(s32[128,2]{0,1:T(2,128)} %param.16) | copy-start | bytes 3076
  7.2 4.6 %copy-start.15 = (s32[16]{0:T(128)S(1)}, s32[16]{0:T(128)}, u32[]{:S(2)}) copy-start(s32[16]{0:T(128)} %param.14) | copy-start | bytes 196
  7.2 4.6 %copy-start.14 = (s32[16]{0:T(128)S(1)}, s32[16]{0:T(128)}, u32[]{:S(2)}) copy-start(s32[16]{0:T(128)} %param.17) | copy-start | bytes 196
  7.2 55.2 %all-gather.3.cloned.1.call-start = ((), (), s32[]{:S(2)}) async-start(), calls=%async_computation.4 | async-start | bytes 6684672 | tf_op jit(solution)/shard_map/all_gather | solution.py:500
  8.6 15.0 %copy-start.13 = (s32[128,2]{0,1:T(2,128)S(1)}, s32[128,2]{0,1:T(2,128)}, u32[]{:S(2)}) copy-start(s32[128,2]{0,1:T(2,128)} %param.19) | copy-start | bytes 3076
  8.6 15.1 %copy-start.16 = (s32[16]{0:T(128)S(1)}, s32[16]{0:T(128)}, u32[]{:S(2)}) copy-start(s32[16]{0:T(128)} %param.20) | copy-start | bytes 196
  8.6 15.3 %copy-start.5 = (bf16[4096,128]{1,0:T(8,128)(2,1)S(1)}, bf16[4096,128]{1,0:T(8,128)(2,1)}, u32[]{:S(2)}) copy-start(bf16[4096,128]{1,0:T(8,128)(2,1)} %param.18) | copy-start | bytes 3145732
  13.6 20.4 %all-to-all-start = ((bf16[16,40,128]{2,1,0:T(8,128)(2,1)}), bf16[16,40,128]{2,1,0:T(8,128)(2,1)S(1)}, u32[]{:S(2)}, u32[]{:S(2)}) async-start(bf16[16,40,128]{2,1,0:T(8,128)(2,1)} %pad_maximum_fusion.4), calls=%async_computation | async-start | bytes 327680 | tf_op jit(solution)/shard_map/all_to_all | solution.py:528
  23.5 135.7 %reduce-scatter.2.cloned.1.call-start = ((), (), s32[]{:S(2)}) async-start(), calls=%async_computation.3 | async-start | bytes 4456448 | tf_op jit(solution)/shard_map/reduce_scatter | solution.py:556
  24.1 19.2 %copy-start.1 = (bf16[128,32,128]{2,1,0:T(8,128)(2,1)}, bf16[128,32,128]{2,1,0:T(8,128)(2,1)S(1)}, u32[]{:S(2)}) copy-start(bf16[128,32,128]{2,1,0:T(8,128)(2,1)S(1)} %broadcast_select_fusion.down) | copy-start | bytes 3145732
  34.7 8.7 %collective-permute-start = (bf16[16,32,128]{2,1,0:T(8,128)(2,1)}, bf16[16,32,128]{2,1,0:T(8,128)(2,1)}, u32[]{:S(2)}, u32[]{:S(2)}) collective-permute-start(bf16[16,32,128]{2,1,0:T(8,128)(2,1)} %get-tuple-element.57), channel_id=1, source_target_pairs={{0,16},{16,32},{32,48},{48,0},{64,80},{80,96},{96,112},{112,64},{1... | collective-permute-start | bytes 393224 | tf_op jit(solution)/shard_map/ppermute | solution.py:448
  35.9 7.5 %collective-permute-start.1 = (bf16[16,32,128]{2,1,0:T(8,128)(2,1)}, bf16[16,32,128]{2,1,0:T(8,128)(2,1)}, u32[]{:S(2)}, u32[]{:S(2)}) collective-permute-start(bf16[16,32,128]{2,1,0:T(8,128)(2,1)} %get-tuple-element.57), channel_id=1, source_target_pairs={{0,32},{16,48},{32,0},{48,16},{64,96},{80,112},{96,64},{112,80},{1... | collective-permute-start | bytes 393224 | tf_op jit(solution)/shard_map/ppermute | solution.py:448
  38.4 5.0 %collective-permute-start.2 = (bf16[16,32,128]{2,1,0:T(8,128)(2,1)}, bf16[16,32,128]{2,1,0:T(8,128)(2,1)}, u32[]{:S(2)}, u32[]{:S(2)}) collective-permute-start(bf16[16,32,128]{2,1,0:T(8,128)(2,1)} %get-tuple-element.57), channel_id=1, source_target_pairs={{0,48},{16,0},{32,16},{48,32},{64,112},{80,64},{96,80},{112,96},{1... | collective-permute-start | bytes 393224 | tf_op jit(solution)/shard_map/ppermute | solution.py:448
  44.5 9.9 %collective-permute-start.3 = (bf16[4,16,32,128]{3,2,1,0:T(8,128)(2,1)S(1)}, bf16[4,16,32,128]{3,2,1,0:T(8,128)(2,1)S(1)}, u32[]{:S(2)}, u32[]{:S(2)}) collective-permute-start(bf16[4,16,32,128]{3,2,1,0:T(8,128)(2,1)S(1)} %pad_maximum_fusion.1.gu_0), channel_id=1, source_target_pairs={{0,64},{64,128},{128,192},{192,0},{16,80},{80,144},{144,208},{208,... | collective-permute-start | bytes 1572872 | tf_op jit(solution)/shard_map/ppermute | solution.py:448
  45.9 15.3 %collective-permute-start.4 = (bf16[4,16,32,128]{3,2,1,0:T(8,128)(2,1)S(1)}, bf16[4,16,32,128]{3,2,1,0:T(8,128)(2,1)}, u32[]{:S(2)}, u32[]{:S(2)}) collective-permute-start(bf16[4,16,32,128]{3,2,1,0:T(8,128)(2,1)S(1)} %pad_maximum_fusion.1.gu_0), channel_id=1, source_target_pairs={{0,128},{64,192},{128,0},{192,64},{16,144},{80,208},{144,16},{208,... | collective-permute-start | bytes 1572872 | tf_op jit(solution)/shard_map/ppermute | solution.py:448
  48.7 12.6 %collective-permute-start.5 = (bf16[4,16,32,128]{3,2,1,0:T(8,128)(2,1)S(1)}, bf16[4,16,32,128]{3,2,1,0:T(8,128)(2,1)}, u32[]{:S(2)}, u32[]{:S(2)}) collective-permute-start(bf16[4,16,32,128]{3,2,1,0:T(8,128)(2,1)S(1)} %pad_maximum_fusion.1.gu_0), channel_id=1, source_target_pairs={{0,192},{64,0},{128,64},{192,128},{16,208},{80,16},{144,80},{208,1... | collective-permute-start | bytes 1572872 | tf_op jit(solution)/shard_map/ppermute | solution.py:448
  74.9 12.5 %copy-start.2 = (bf16[4,24,32,128]{3,2,1,0:T(8,128)(2,1)}, bf16[4,24,32,128]{3,2,1,0:T(8,128)(2,1)S(1)}, u32[]{:S(2)}) copy-start(bf16[4,24,32,128]{3,2,1,0:T(8,128)(2,1)S(1)} %get-tuple-element.42) | copy-start | bytes 2359300
  74.9 12.5 %collective-permute-start.6 = (bf16[4,24,32,128]{3,2,1,0:T(8,128)(2,1)S(1)}, bf16[4,24,32,128]{3,2,1,0:T(8,128)(2,1)S(1)}, u32[]{:S(2)}, u32[]{:S(2)}) collective-permute-start(bf16[4,24,32,128]{3,2,1,0:T(8,128)(2,1)S(1)} %get-tuple-element.35), channel_id=1, source_target_pairs={{0,64},{64,128},{128,192},{192,0},{16,80},{80,144},{144,208},{208,... | collective-permute-start | bytes 2359304 | tf_op jit(solution)/shard_map/ppermute | solution.py:448
  76.2 20.8 %collective-permute-start.7 = (bf16[4,24,32,128]{3,2,1,0:T(8,128)(2,1)S(1)}, bf16[4,24,32,128]{3,2,1,0:T(8,128)(2,1)S(1)}, u32[]{:S(2)}, u32[]{:S(2)}) collective-permute-start(bf16[4,24,32,128]{3,2,1,0:T(8,128)(2,1)S(1)} %get-tuple-element.36), channel_id=1, source_target_pairs={{0,128},{64,192},{128,0},{192,64},{16,144},{80,208},{144,16},{208,... | collective-permute-start | bytes 2359304 | tf_op jit(solution)/shard_map/ppermute | solution.py:448
  78.9 18.1 %collective-permute-start.8 = (bf16[4,24,32,128]{3,2,1,0:T(8,128)(2,1)S(1)}, bf16[4,24,32,128]{3,2,1,0:T(8,128)(2,1)S(1)}, u32[]{:S(2)}, u32[]{:S(2)}) collective-permute-start(bf16[4,24,32,128]{3,2,1,0:T(8,128)(2,1)S(1)} %get-tuple-element.37), channel_id=1, source_target_pairs={{0,192},{64,0},{128,64},{192,128},{16,208},{80,16},{144,80},{208,1... | collective-permute-start | bytes 2359304 | tf_op jit(solution)/shard_map/ppermute | solution.py:448
  87.4 9.6 %copy-start.6 = (bf16[4,24,32,128]{3,2,1,0:T(8,128)(2,1)}, bf16[4,24,32,128]{3,2,1,0:T(8,128)(2,1)S(1)}, u32[]{:S(2)}) copy-start(bf16[4,24,32,128]{3,2,1,0:T(8,128)(2,1)S(1)} %collective-permute-done.6) | copy-start | bytes 2359300
  97.0 0.9 copy-start.8
  97.0 1.1 copy-start.10
  98.1 1.1 copy-start.3
  98.1 1.4 copy-start.7
  98.1 1.6 copy-start.9
  101.3 6.4 %collective-permute-start.10 = (bf16[24,32,128]{2,1,0:T(8,128)(2,1)S(1)}, bf16[24,32,128]{2,1,0:T(8,128)(2,1)S(1)}, u32[]{:S(2)}, u32[]{:S(2)}) collective-permute-start(bf16[24,32,128]{2,1,0:T(8,128)(2,1)S(1)} %get-tuple-element.53), channel_id=1, source_target_pairs={{0,32},{16,48},{32,0},{48,16},{64,96},{80,112},{96,64},{112,80},{1... | collective-permute-start | bytes 589832 | tf_op jit(solution)/shard_map/ppermute | solution.py:448
  103.9 5.7 %collective-permute-start.11 = (bf16[24,32,128]{2,1,0:T(8,128)(2,1)S(1)}, bf16[24,32,128]{2,1,0:T(8,128)(2,1)S(1)}, u32[]{:S(2)}, u32[]{:S(2)}) collective-permute-start(bf16[24,32,128]{2,1,0:T(8,128)(2,1)S(1)} %get-tuple-element.52), channel_id=1, source_target_pairs={{0,48},{16,0},{32,16},{48,32},{64,112},{80,64},{96,80},{112,96},{1... | collective-permute-start | bytes 589832 | tf_op jit(solution)/shard_map/ppermute | solution.py:448
  104.7 5.7 %collective-permute-start.9 = (bf16[24,32,128]{2,1,0:T(8,128)(2,1)S(1)}, bf16[24,32,128]{2,1,0:T(8,128)(2,1)S(1)}, u32[]{:S(2)}, u32[]{:S(2)}) collective-permute-start(bf16[24,32,128]{2,1,0:T(8,128)(2,1)S(1)} %get-tuple-element.51), channel_id=1, source_target_pairs={{0,16},{16,32},{32,48},{48,0},{64,80},{80,96},{96,112},{112,64},{1... | collective-permute-start | bytes 589832 | tf_op jit(solution)/shard_map/ppermute | solution.py:448
  111.3 17.3 %all-to-all-start.1 = ((bf16[16,32,128]{2,1,0:T(8,128)(2,1)}), bf16[16,32,128]{2,1,0:T(8,128)(2,1)S(1)}, u32[]{:S(2)}, u32[]{:S(2)}) async-start(bf16[16,32,128]{2,1,0:T(8,128)(2,1)} %slice.48), calls=%async_computation.2 | async-start | bytes 262144 | tf_op jit(solution)/shard_map/all_to_all | solution.py:561
  128.7 6.1 %collective-permute-start.12 = (bf16[24,32,128]{2,1,0:T(8,128)(2,1)S(1)}, bf16[24,32,128]{2,1,0:T(8,128)(2,1)S(1)}, u32[]{:S(2)}, u32[]{:S(2)}) collective-permute-start(bf16[24,32,128]{2,1,0:T(8,128)(2,1)S(1)} %get-tuple-element.55), channel_id=1, source_target_pairs={{0,16},{16,32},{32,48},{48,0},{64,80},{80,96},{96,112},{112,64},{1... | collective-permute-start | bytes 589832 | tf_op jit(solution)/shard_map/ppermute | solution.py:448
  130.1 7.0 %collective-permute-start.13 = (bf16[24,32,128]{2,1,0:T(8,128)(2,1)S(1)}, bf16[24,32,128]{2,1,0:T(8,128)(2,1)S(1)}, u32[]{:S(2)}, u32[]{:S(2)}) collective-permute-start(bf16[24,32,128]{2,1,0:T(8,128)(2,1)S(1)} %get-tuple-element.55), channel_id=1, source_target_pairs={{0,32},{16,48},{32,0},{48,16},{64,96},{80,112},{96,64},{112,80},{1... | collective-permute-start | bytes 589832 | tf_op jit(solution)/shard_map/ppermute | solution.py:448
  131.9 5.6 %collective-permute-start.14 = (bf16[24,32,128]{2,1,0:T(8,128)(2,1)S(1)}, bf16[24,32,128]{2,1,0:T(8,128)(2,1)S(1)}, u32[]{:S(2)}, u32[]{:S(2)}) collective-permute-start(bf16[24,32,128]{2,1,0:T(8,128)(2,1)S(1)} %get-tuple-element.55), channel_id=1, source_target_pairs={{0,48},{16,0},{32,16},{48,32},{64,112},{80,64},{96,80},{112,96},{1... | collective-permute-start | bytes 589832 | tf_op jit(solution)/shard_map/ppermute | solution.py:448
  137.6 20.8 %collective-permute-start.15 = (bf16[4,24,32,128]{3,2,1,0:T(8,128)(2,1)S(1)}, bf16[4,24,32,128]{3,2,1,0:T(8,128)(2,1)S(1)}, u32[]{:S(2)}, u32[]{:S(2)}) collective-permute-start(bf16[4,24,32,128]{3,2,1,0:T(8,128)(2,1)S(1)} %pad_maximum_fusion.full_0), channel_id=1, source_target_pairs={{0,64},{64,128},{128,192},{192,0},{16,80},{80,144},{144,208},{208,... | collective-permute-start | bytes 2359304 | tf_op jit(solution)/shard_map/ppermute | solution.py:448
  137.7 20.8 %collective-permute-start.16 = (bf16[4,24,32,128]{3,2,1,0:T(8,128)(2,1)S(1)}, bf16[4,24,32,128]{3,2,1,0:T(8,128)(2,1)S(1)}, u32[]{:S(2)}, u32[]{:S(2)}) collective-permute-start(bf16[4,24,32,128]{3,2,1,0:T(8,128)(2,1)S(1)} %pad_maximum_fusion.full_0), channel_id=1, source_target_pairs={{0,128},{64,192},{128,0},{192,64},{16,144},{80,208},{144,16},{208,... | collective-permute-start | bytes 2359304 | tf_op jit(solution)/shard_map/ppermute | solution.py:448
  139.8 19.3 %collective-permute-start.17 = (bf16[4,24,32,128]{3,2,1,0:T(8,128)(2,1)S(1)}, bf16[4,24,32,128]{3,2,1,0:T(8,128)(2,1)S(1)}, u32[]{:S(2)}, u32[]{:S(2)}) collective-permute-start(bf16[4,24,32,128]{3,2,1,0:T(8,128)(2,1)S(1)} %pad_maximum_fusion.full_0), channel_id=1, source_target_pairs={{0,192},{64,0},{128,64},{192,128},{16,208},{80,16},{144,80},{208,1... | collective-permute-start | bytes 2359304 | tf_op jit(solution)/shard_map/ppermute | solution.py:448
  159.2 0.9 copy-start.4
Sparse Core Ops, SparseCore 0:
  10.8 51.5 all-gather.2
  98.3 60.8 reduce-scatter.1

commit v3 on v2

--- a/solution.py
+++ b/solution.py
@@ -274,37 +274,32 @@
         store(n).wait()
 
 
-def turn_back(summed, layer_output, grad_tokens, ordered):
+def turn_back_kernel(summed, layer_output, grad_tokens, held, ordered, sems):
     width = D_OWN * TILE
+
+    def load(half):
+        rows = pl.ds(half * width, width)
+        return pltpu.make_async_copy(summed.at[rows], held.at[rows], sems.at[half])
+
+    load(1).start()
+    load(0).start()
+    load(1).wait()
     for r in range(D_OWN):
         for odd in range(2):
-            rows = summed[pl.ds(width + r * TILE + odd * HALF, HALF), :]
+            rows = held[pl.ds(width + r * TILE + odd * HALF, HALF), :]
             ordered[pl.ds(r * TILE + odd, HALF, stride=2), :] = rows.astype(F32)
     for n in range(width // 128):
         lanes = pl.ds(n * 128, 128)
-        layer_output[:, lanes] = summed[lanes, :].T
         grad_tokens[:, lanes] = ordered[lanes, :].T.astype(BF)
-
-
-def finish_kernel(
-    place,
-    summed,
-    full_0,
-    full_1,
-    full_2,
-    full_3,
-    layer_output,
-    grad_tokens,
-    gate,
-    up,
-    down,
-    ordered,
-    sems,
-):
+    load(0).wait()
+    for n in range(width // 128):
+        lanes = pl.ds(n * 128, 128)
+        layer_output[:, lanes] = held[lanes, :].T
+
+
+def place_kernel(place, full_0, full_1, full_2, full_3, gate, up, down, sems):
     full = (full_0, full_1, full_2, full_3)
     for phase in range(2):
-        if phase == 1:
-            turn_back(summed, layer_output, grad_tokens, ordered)
         for k in range(SIDE):
             first = (place[0] + SIDE - k) & (SIDE - 1)
             for j in range(SIDE):
@@ -404,20 +399,37 @@
     )(place, meta, dmeta, down_t, hidden_split, pre, *gu)
 
 
-def finish(place, summed, full):
+def place_grads(place, full):
     tiles = jax.ShapeDtypeStruct((GROUPS, DEPTH, HALF, 128), BF)
+    return pl.pallas_call(
+        place_kernel,
+        out_shape=(tiles,) * 3,
+        in_specs=[SMEM] + [ANY] * SIDE,
+        out_specs=(ANY,) * 3,
+        scratch_shapes=[pltpu.SemaphoreType.DMA((2, SIDE * SIDE))],
+        compiler_params=pltpu.CompilerParams(vmem_limit_bytes=SMALL),
+        cost_estimate=pl.CostEstimate(flops=0, bytes_accessed=2**22, transcendentals=0),
+        name="place_kernel",
+    )(place, *full)
+
+
+def turn_back(summed):
     width = D_OWN * TILE
     rows = jax.ShapeDtypeStruct((128, width), BF)
     return pl.pallas_call(
-        finish_kernel,
-        out_shape=(rows,) * 2 + (tiles,) * 3,
-        in_specs=[SMEM, VMEM] + [ANY] * SIDE,
-        out_specs=(VMEM,) * 2 + (ANY,) * 3,
-        scratch_shapes=[pltpu.VMEM((width, 128), F32), pltpu.SemaphoreType.DMA((2, SIDE * SIDE))],
-        compiler_params=pltpu.CompilerParams(vmem_limit_bytes=SMALL),
-        cost_estimate=pl.CostEstimate(flops=0, bytes_accessed=2**22, transcendentals=0),
-        name="finish_kernel",
-    )(place, summed, *full)
+        turn_back_kernel,
+        out_shape=(rows,) * 2,
+        in_specs=[ANY],
+        out_specs=(VMEM,) * 2,
+        scratch_shapes=[
+            pltpu.VMEM((2 * width, 128), BF),
+            pltpu.VMEM((width, 128), F32),
+            pltpu.SemaphoreType.DMA((2,)),
+        ],
+        compiler_params=pltpu.CompilerParams(vmem_limit_bytes=60 * 1024 * 1024),
+        cost_estimate=pl.CostEstimate(flops=0, bytes_accessed=2**19, transcendentals=0),
+        name="turn_back_kernel",
+    )(summed)
 
 
 def split_order(size):
@@ -461,7 +473,10 @@
         for k in range(SIDE)
     ]
     got = [ahead[0]] + [shift(ahead[k], True, k) for k in range(1, SIDE)]
-    return sum(part.astype(F32) for part in got).astype(BF)
+    return [
+        sum(part[rows].astype(F32) for part in got).astype(BF)
+        for rows in (slice(0, GROUPS), slice(GROUPS, None))
+    ]
 
 
 def per_device(
@@ -557,11 +572,12 @@
         partials.reshape(GROUPS * 2 * width, 128), "mp", scatter_dimension=0, tiled=True
     )
 
-    got = from_replicas(grads, part % SIDE)
-    back = lax.all_to_all(got[:GROUPS], "mp", 0, 0, tiled=True)
-    piece = jnp.concatenate([jnp.where(my_live, back, 0), got[GROUPS:]], axis=0)
+    got_gu, got_down = from_replicas(grads, part % SIDE)
+    back = lax.all_to_all(got_gu, "mp", 0, 0, tiled=True)
+    piece = jnp.concatenate([jnp.where(my_live, back, 0), got_down], axis=0)
     flat = (GROUPS * DEPTH * HALF, 128)
-    layer_output, grad_tokens, *tile_grads = finish(place, summed, to_replicas(piece))
+    tile_grads = place_grads(place, to_replicas(piece))
+    layer_output, grad_tokens = turn_back(summed)
     grad_gate, grad_up, grad_down = (g.reshape(flat) for g in tile_grads)
     return (layer_output, grad_tokens, grad_gate, grad_up, grad_down)
 

time: 173 us -> 172 us (level)
    pallas_call x1 -> x2, Pallas kernels: 3.17 us -> 4.24 us  [the longest x1 2.46 us: place_grads(): pl.pallas_call(place_kernel, out_shape=(tiles,) * 3, in_specs=[SMEM] + [A...]
    unnamed x36 -> x34, local copies, waits for them, and re-layouts: 4.59 us -> 3.63 us
  transfers between devices with their start and end apart: 22 -> 22, of which waited for: 14 -> 14; matrix products, arithmetic and copies ran while one was open for 5% -> 5% of each run, Pallas kernels for 6% -> 8%
where the time goes in v3:
time: 172 us; the launch traced here: 170 us
  waiting for transfers between devices  69.5 us (40%)
  starting transfers between devices  44.3 us (26%)
  Pallas kernels  27.4 us (16%)
  between operations  14.6 us (8%)
  other arithmetic  6.76 us (4%)
  local copies, waits for them, and re-layouts  5.95 us (3%)
    ppermute x18, waiting for transfers between devices, shift(): return lax.ppermute(value, ('dp', 'mp'), pairs)  48.7 us
    ppermute x18, starting transfers between devices, shift(): return lax.ppermute(value, ('dp', 'mp'), pairs)  26.8 us
    pallas_call x1, Pallas kernels, layer(): pl.pallas_call(layer_kernel, out_shape=(piece,) * SIDE + (jax.ShapeDtypeS...  12.4 us
    all_to_all x1, starting transfers between devices, per_device(): lax.all_to_all(jnp.concatenate([mine, notes], axis=1), 'mp', 0, 0, tiled=...  9.98 us
    all_to_all x1, waiting for transfers between devices, per_device(): lax.all_to_all(jnp.concatenate([mine, notes], axis=1), 'mp', 0, 0, tiled=...  9.85 us
    all_to_all x1, waiting for transfers between devices, per_device(): back = lax.all_to_all(got_gu, 'mp', 0, 0, tiled=True)  9.79 us
    all_to_all x1, starting transfers between devices, per_device(): back = lax.all_to_all(got_gu, 'mp', 0, 0, tiled=True)  7.47 us
    pallas_call x1, Pallas kernels, output_part(): pl.pallas_call(output_kernel, out_shape=jax.ShapeDtypeStruct((GROUPS, 2,...  7.4 us
  transfers between devices with their start and end apart: 22, of which 14 were waited for; matrix products, arithmetic and copies ran while one was open for 5% of the time, Pallas kernels for 8%

profile of v3, /device:TPU:1, one launch (start us, length us, event | category | flops | bytes accessed | tf_op | source)
XLA Modules:
  0.0 170.2 jit_solution(16865533224184548667)
XLA Ops:
  7.3 0.8 copy-done
  8.1 0.4 convolution_convert_fusion.1
  8.4 0.1 copy.37
  8.6 1.3 convolution_convert_fusion
  9.9 0.8 pad_maximum_fusion.2
  11.1 0.1 copy.44
  11.2 0.1 copy.45
  11.5 0.1 copy.46
  11.7 0.1 fusion.17
  11.8 1.1 fusion.5
  12.9 0.7 pad_maximum_fusion.4
  13.6 10.0 %all-to-all-start = ((bf16[16,40,128]{2,1,0:T(8,128)(2,1)}), bf16[16,40,128]{2,1,0:T(8,128)(2,1)S(1)}, u32[]{:S(2)}, u32[]{:S(2)}) async-start(bf16[16,40,128]{2,1,0:T(8,128)(2,1)} %pad_maximum_fusion.4), calls=%async_computation | async-start | bytes 327680 | tf_op jit(solution)/shard_map/all_to_all | solution.py:543
  23.8 0.1 lt.117
  23.9 0.2 broadcast_select_fusion.down
  24.1 9.8 %all-to-all-done = bf16[16,40,128]{2,1,0:T(8,128)(2,1)S(1)} async-done(((bf16[16,40,128]{2,1,0:T(8,128)(2,1)}), bf16[16,40,128]{2,1,0:T(8,128)(2,1)S(1)}, u32[]{:S(2)}, u32[]{:S(2)}) %all-to-all-start) | async-done | bytes 163872 | tf_op jit(solution)/shard_map/all_to_all | solution.py:543
  34.0 0.7 slice_bitcast_fusion
  34.7 1.2 collective-permute-start
  35.9 2.5 %collective-permute-start.1 = (bf16[16,32,128]{2,1,0:T(8,128)(2,1)}, bf16[16,32,128]{2,1,0:T(8,128)(2,1)}, u32[]{:S(2)}, u32[]{:S(2)}) collective-permute-start(bf16[16,32,128]{2,1,0:T(8,128)(2,1)} %get-tuple-element.57), channel_id=1, source_target_pairs={{0,32},{16,48},{32,0},{48,16},{64,96},{80,112},{96,64},{112,80},{1... | collective-permute-start | bytes 393224 | tf_op jit(solution)/shard_map/ppermute | solution.py:460
  38.4 1.2 collective-permute-start.2
  39.7 0.1 sub.120
  39.8 0.1 sub.118
  39.9 0.1 reshape.326
  40.0 3.3 %turn_kernel.1.down_t = bf16[128,64,64]{2,1,0:T(8,128)(2,1)S(1)} custom-call(bf16[128,32,128]{2,1,0:T(8,128)(2,1)S(1)} %broadcast_select_fusion.down), custom_call_target="tpu_custom_call" | custom-call | flops 67108864 | bytes 4194304 | tf_op jit(solution)/shard_map/turn_kernel/pallas_call | solution.py:339
  43.4 1.2 pad_maximum_fusion.1.gu_0
  44.5 1.4 collective-permute-start.3
  45.9 2.8 %collective-permute-start.4 = (bf16[4,16,32,128]{3,2,1,0:T(8,128)(2,1)S(1)}, bf16[4,16,32,128]{3,2,1,0:T(8,128)(2,1)}, u32[]{:S(2)}, u32[]{:S(2)}) collective-permute-start(bf16[4,16,32,128]{3,2,1,0:T(8,128)(2,1)S(1)} %pad_maximum_fusion.1.gu_0), channel_id=1, source_target_pairs={{0,128},{64,192},{128,0},{192,64},{16,144},{80,208},{144,16},{208,... | collective-permute-start | bytes 1572872 | tf_op jit(solution)/shard_map/ppermute | solution.py:460
  48.7 1.0 collective-permute-start.5
  50.0 4.5 %collective-permute-done.3.gu_1 = bf16[4,16,32,128]{3,2,1,0:T(8,128)(2,1)S(1)} collective-permute-done((bf16[4,16,32,128]{3,2,1,0:T(8,128)(2,1)S(1)}, bf16[4,16,32,128]{3,2,1,0:T(8,128)(2,1)S(1)}, u32[]{:S(2)}, u32[]{:S(2)}) %collective-permute-start.3) | collective-permute-done | bytes 524320 | tf_op jit(solution)/shard_map/ppermute | solution.py:460
  54.5 6.8 %collective-permute-done.4.gu_2 = bf16[4,16,32,128]{3,2,1,0:T(8,128)(2,1)} collective-permute-done((bf16[4,16,32,128]{3,2,1,0:T(8,128)(2,1)S(1)}, bf16[4,16,32,128]{3,2,1,0:T(8,128)(2,1)}, u32[]{:S(2)}, u32[]{:S(2)}) %collective-permute-start.4) | collective-permute-done | bytes 524320 | tf_op jit(solution)/shard_map/ppermute | solution.py:460
  61.3 1.1 all-gather.3.cloned.1.call-done
  62.4 12.4 %layer_kernel.1 = (bf16[4,24,32,128]{3,2,1,0:T(8,128)(2,1)S(1)}, bf16[4,24,32,128]{3,2,1,0:T(8,128)(2,1)S(1)}, bf16[4,24,32,128]{3,2,1,0:T(8,128)(2,1)S(1)}, bf1...) custom-call(s32[2]{0:T(128)S(1)} %pad_add_fusion.1.place, ...), custom_call_target="tpu_custom_call" | custom-call | flops 536870912 | bytes 8388608 | tf_op jit(solution)/shard_map/layer_kernel/pallas_call | solution.py:354
  74.9 1.3 collective-permute-start.6
  76.2 2.7 %collective-permute-start.7 = (bf16[4,24,32,128]{3,2,1,0:T(8,128)(2,1)S(1)}, bf16[4,24,32,128]{3,2,1,0:T(8,128)(2,1)S(1)}, u32[]{:S(2)}, u32[]{:S(2)}) collective-permute-start(bf16[4,24,32,128]{3,2,1,0:T(8,128)(2,1)S(1)} %get-tuple-element.36), channel_id=1, source_target_pairs={{0,128},{64,192},{128,0},{192,64},{16,144},{80,208},{144,16},{208,... | collective-permute-start | bytes 2359304 | tf_op jit(solution)/shard_map/ppermute | solution.py:460
  78.9 1.0 collective-permute-start.8
  79.9 7.4 %output_kernel.1 = bf16[16,2,8,64,128]{4,3,2,1,0:T(8,128)(2,1)} custom-call(s32[2]{0:T(128)S(1)} %pad_add_fusion.1.place, s32[16,32]{1,0:T(8,128)S(1)} %copy.50.meta, s32[3,128]{1,0:T(4,128)S(1)} %pad_add_fusion.dmeta, bf16[128,64,64]{2,1,0:T(8,128)(2,1)S(1)} %turn_kernel.1.down_t, bf16[14,64,128]{2,1,0:T(8,128)(2,1)S(1)} %get-tuple-element.39.hidden_split, ...), custom_call_target="tpu_custom_call" | custom-call | flops 268435456 | bytes 8388608 | tf_op jit(solution)/shard_map/output_kernel/pallas_call | solution.py:383
  87.4 9.6 %collective-permute-done.7 = bf16[4,24,32,128]{3,2,1,0:T(8,128)(2,1)S(1)} collective-permute-done((bf16[4,24,32,128]{3,2,1,0:T(8,128)(2,1)S(1)}, bf16[4,24,32,128]{3,2,1,0:T(8,128)(2,1)S(1)}, u32[]{:S(2)}, u32[]{:S(2)}) %collective-permute-start.7) | collective-permute-done | bytes 786464 | tf_op jit(solution)/shard_map/ppermute | solution.py:460
  97.0 0.9 copy-done.7
  97.9 0.3 copy-done.9
  98.2 1.0 copy-done.3
  99.3 0.2 copy-done.6
  99.5 0.2 copy-done.8
  99.7 1.5 add_convert_fusion
  101.3 2.5 %collective-permute-start.10 = (bf16[24,32,128]{2,1,0:T(8,128)(2,1)S(1)}, bf16[24,32,128]{2,1,0:T(8,128)(2,1)S(1)}, u32[]{:S(2)}, u32[]{:S(2)}) collective-permute-start(bf16[24,32,128]{2,1,0:T(8,128)(2,1)S(1)} %get-tuple-element.53), channel_id=1, source_target_pairs={{0,32},{16,48},{32,0},{48,16},{64,96},{80,112},{96,64},{112,80},{1... | collective-permute-start | bytes 589832 | tf_op jit(solution)/shard_map/ppermute | solution.py:460
  103.8 0.9 collective-permute-start.11
  104.7 0.6 collective-permute-start.9
  105.3 2.4 %collective-permute-done.10 = bf16[24,32,128]{2,1,0:T(8,128)(2,1)S(1)} collective-permute-done((bf16[24,32,128]{2,1,0:T(8,128)(2,1)S(1)}, bf16[24,32,128]{2,1,0:T(8,128)(2,1)S(1)}, u32[]{:S(2)}, u32[]{:S(2)}) %collective-permute-start.10) | collective-permute-done | bytes 196640 | tf_op jit(solution)/shard_map/ppermute | solution.py:460
  107.7 1.9 %collective-permute-done.11 = bf16[24,32,128]{2,1,0:T(8,128)(2,1)S(1)} collective-permute-done((bf16[24,32,128]{2,1,0:T(8,128)(2,1)S(1)}, bf16[24,32,128]{2,1,0:T(8,128)(2,1)S(1)}, u32[]{:S(2)}, u32[]{:S(2)}) %collective-permute-start.11) | collective-permute-done | bytes 196640 | tf_op jit(solution)/shard_map/ppermute | solution.py:460
  109.6 0.8 collective-permute-done.9
  110.4 0.7 fusion.3
  111.2 7.5 %all-to-all-start.1 = ((bf16[16,32,128]{2,1,0:T(8,128)(2,1)}), bf16[16,32,128]{2,1,0:T(8,128)(2,1)S(1)}, u32[]{:S(2)}, u32[]{:S(2)}) async-start(bf16[16,32,128]{2,1,0:T(8,128)(2,1)} %fusion.3), calls=%async_computation.2 | async-start | bytes 262144 | tf_op jit(solution)/shard_map/all_to_all | solution.py:576
  118.7 9.8 %all-to-all-done.1 = bf16[16,32,128]{2,1,0:T(8,128)(2,1)S(1)} async-done(((bf16[16,32,128]{2,1,0:T(8,128)(2,1)}), bf16[16,32,128]{2,1,0:T(8,128)(2,1)S(1)}, u32[]{:S(2)}, u32[]{:S(2)}) %all-to-all-start.1) | async-done | bytes 131104 | tf_op jit(solution)/shard_map/all_to_all | solution.py:576
  128.6 1.5 collective-permute-start.12
  130.1 1.7 %collective-permute-start.13 = (bf16[24,32,128]{2,1,0:T(8,128)(2,1)S(1)}, bf16[24,32,128]{2,1,0:T(8,128)(2,1)S(1)}, u32[]{:S(2)}, u32[]{:S(2)}) collective-permute-start(bf16[24,32,128]{2,1,0:T(8,128)(2,1)S(1)} %get-tuple-element.55), channel_id=1, source_target_pairs={{0,32},{16,48},{32,0},{48,16},{64,96},{80,112},{96,64},{112,80},{1... | collective-permute-start | bytes 589832 | tf_op jit(solution)/shard_map/ppermute | solution.py:460
  131.8 1.3 collective-permute-start.14
  133.1 1.6 collective-permute-done.12
  134.7 2.3 %collective-permute-done.13 = bf16[24,32,128]{2,1,0:T(8,128)(2,1)S(1)} collective-permute-done((bf16[24,32,128]{2,1,0:T(8,128)(2,1)S(1)}, bf16[24,32,128]{2,1,0:T(8,128)(2,1)S(1)}, u32[]{:S(2)}, u32[]{:S(2)}) %collective-permute-start.13) | collective-permute-done | bytes 196640 | tf_op jit(solution)/shard_map/ppermute | solution.py:460
  137.0 0.4 collective-permute-done.14
  137.4 0.1 pad_maximum_fusion.full_0
  137.6 2.1 %collective-permute-start.16 = (bf16[4,24,32,128]{3,2,1,0:T(8,128)(2,1)S(1)}, bf16[4,24,32,128]{3,2,1,0:T(8,128)(2,1)S(1)}, u32[]{:S(2)}, u32[]{:S(2)}) collective-permute-start(bf16[4,24,32,128]{3,2,1,0:T(8,128)(2,1)S(1)} %pad_maximum_fusion.full_0), channel_id=1, source_target_pairs={{0,128},{64,192},{128,0},{192,64},{16,144},{80,208},{144,16},{208,... | collective-permute-start | bytes 2359304 | tf_op jit(solution)/shard_map/ppermute | solution.py:460
  139.7 1.1 collective-permute-start.17
  140.7 17.6 %collective-permute-done.15.full_1 = bf16[4,24,32,128]{3,2,1,0:T(8,128)(2,1)S(1)} collective-permute-done((bf16[4,24,32,128]{3,2,1,0:T(8,128)(2,1)S(1)}, bf16[4,24,32,128]{3,2,1,0:T(8,128)(2,1)S(1)}, u32[]{:S(2)}, u32[]{:S(2)}) %collective-permute-start.15) | collective-permute-done | bytes 786464 | tf_op jit(solution)/shard_map/ppermute | solution.py:460
  158.3 0.7 collective-permute-done.17.full_3
  159.1 2.5 %place_kernel.1 = (bf16[16,8,32,128]{3,2,1,0:T(8,128)(2,1)}, bf16[16,8,32,128]{3,2,1,0:T(8,128)(2,1)}, bf16[16,8,32,128]{3,2,1,0:T(8,128)(2,1)}) custom-call(s32[2]{0:T(128)S(1)} %pad_add_fusion.1.place, bf16[4,24,32,128]{3,2,1,0:T(8,128)(2,1)S(1)} %pad_maximum_fusion.full_0, bf16[4,24,32,128]{3,2,1,0:T(8,128)(2,1)S(1)} %collective-permute-done.15.full_1, ...), custom_call_target="tpu_custom_call" | custom-call | bytes 4194304 | tf_op jit(solution)/shard_map/place_kernel/pallas_call | solution.py:404
  161.6 1.8 %turn_back_kernel.1 = (bf16[128,512]{1,0:T(8,128)(2,1)}, bf16[128,512]{1,0:T(8,128)(2,1)}) custom-call(bf16[1024,128]{1,0:T(8,128)(2,1)} %reduce-scatter.2.cloned.1.call-done.summed), custom_call_target="tpu_custom_call" | custom-call | bytes 524288 | tf_op jit(solution)/shard_map/turn_back_kernel/pallas_call | solution.py:419
  (71 shorter events, 1.7 us)
Async XLA Ops:
  7.2 0.9 copy-start
  7.2 3.6 %copy-start.10 = (s32[128,2]{0,1:T(2,128)S(1)}, s32[128,2]{0,1:T(2,128)}, u32[]{:S(2)}) copy-start(s32[128,2]{0,1:T(2,128)} %param.13) | copy-start | bytes 3076
  7.2 3.8 %copy-start.11 = (s32[128,2]{0,1:T(2,128)S(1)}, s32[128,2]{0,1:T(2,128)}, u32[]{:S(2)}) copy-start(s32[128,2]{0,1:T(2,128)} %param.16) | copy-start | bytes 3076
  7.2 4.6 %copy-start.14 = (s32[16]{0:T(128)S(1)}, s32[16]{0:T(128)}, u32[]{:S(2)}) copy-start(s32[16]{0:T(128)} %param.14) | copy-start | bytes 196
  7.2 4.6 %copy-start.13 = (s32[16]{0:T(128)S(1)}, s32[16]{0:T(128)}, u32[]{:S(2)}) copy-start(s32[16]{0:T(128)} %param.17) | copy-start | bytes 196
  7.2 55.2 %all-gather.3.cloned.1.call-start = ((), (), s32[]{:S(2)}) async-start(), calls=%async_computation.4 | async-start | bytes 6684672 | tf_op jit(solution)/shard_map/all_gather | solution.py:515
  8.6 15.0 %copy-start.12 = (s32[128,2]{0,1:T(2,128)S(1)}, s32[128,2]{0,1:T(2,128)}, u32[]{:S(2)}) copy-start(s32[128,2]{0,1:T(2,128)} %param.19) | copy-start | bytes 3076
  8.6 15.1 %copy-start.15 = (s32[16]{0:T(128)S(1)}, s32[16]{0:T(128)}, u32[]{:S(2)}) copy-start(s32[16]{0:T(128)} %param.20) | copy-start | bytes 196
  8.6 15.3 %copy-start.4 = (bf16[4096,128]{1,0:T(8,128)(2,1)S(1)}, bf16[4096,128]{1,0:T(8,128)(2,1)}, u32[]{:S(2)}) copy-start(bf16[4096,128]{1,0:T(8,128)(2,1)} %param.18) | copy-start | bytes 3145732
  13.6 20.4 %all-to-all-start = ((bf16[16,40,128]{2,1,0:T(8,128)(2,1)}), bf16[16,40,128]{2,1,0:T(8,128)(2,1)S(1)}, u32[]{:S(2)}, u32[]{:S(2)}) async-start(bf16[16,40,128]{2,1,0:T(8,128)(2,1)} %pad_maximum_fusion.4), calls=%async_computation | async-start | bytes 327680 | tf_op jit(solution)/shard_map/all_to_all | solution.py:543
  23.5 138.0 %reduce-scatter.2.cloned.1.call-start = ((), (), s32[]{:S(2)}) async-start(), calls=%async_computation.3 | async-start | bytes 4456448 | tf_op jit(solution)/shard_map/reduce_scatter | solution.py:571
  24.1 19.2 %copy-start.1 = (bf16[128,32,128]{2,1,0:T(8,128)(2,1)}, bf16[128,32,128]{2,1,0:T(8,128)(2,1)S(1)}, u32[]{:S(2)}) copy-start(bf16[128,32,128]{2,1,0:T(8,128)(2,1)S(1)} %broadcast_select_fusion.down) | copy-start | bytes 3145732
  34.7 8.7 %collective-permute-start = (bf16[16,32,128]{2,1,0:T(8,128)(2,1)}, bf16[16,32,128]{2,1,0:T(8,128)(2,1)}, u32[]{:S(2)}, u32[]{:S(2)}) collective-permute-start(bf16[16,32,128]{2,1,0:T(8,128)(2,1)} %get-tuple-element.57), channel_id=1, source_target_pairs={{0,16},{16,32},{32,48},{48,0},{64,80},{80,96},{96,112},{112,64},{1... | collective-permute-start | bytes 393224 | tf_op jit(solution)/shard_map/ppermute | solution.py:460
  35.9 7.5 %collective-permute-start.1 = (bf16[16,32,128]{2,1,0:T(8,128)(2,1)}, bf16[16,32,128]{2,1,0:T(8,128)(2,1)}, u32[]{:S(2)}, u32[]{:S(2)}) collective-permute-start(bf16[16,32,128]{2,1,0:T(8,128)(2,1)} %get-tuple-element.57), channel_id=1, source_target_pairs={{0,32},{16,48},{32,0},{48,16},{64,96},{80,112},{96,64},{112,80},{1... | collective-permute-start | bytes 393224 | tf_op jit(solution)/shard_map/ppermute | solution.py:460
  38.4 5.0 %collective-permute-start.2 = (bf16[16,32,128]{2,1,0:T(8,128)(2,1)}, bf16[16,32,128]{2,1,0:T(8,128)(2,1)}, u32[]{:S(2)}, u32[]{:S(2)}) collective-permute-start(bf16[16,32,128]{2,1,0:T(8,128)(2,1)} %get-tuple-element.57), channel_id=1, source_target_pairs={{0,48},{16,0},{32,16},{48,32},{64,112},{80,64},{96,80},{112,96},{1... | collective-permute-start | bytes 393224 | tf_op jit(solution)/shard_map/ppermute | solution.py:460
  44.5 9.9 %collective-permute-start.3 = (bf16[4,16,32,128]{3,2,1,0:T(8,128)(2,1)S(1)}, bf16[4,16,32,128]{3,2,1,0:T(8,128)(2,1)S(1)}, u32[]{:S(2)}, u32[]{:S(2)}) collective-permute-start(bf16[4,16,32,128]{3,2,1,0:T(8,128)(2,1)S(1)} %pad_maximum_fusion.1.gu_0), channel_id=1, source_target_pairs={{0,64},{64,128},{128,192},{192,0},{16,80},{80,144},{144,208},{208,... | collective-permute-start | bytes 1572872 | tf_op jit(solution)/shard_map/ppermute | solution.py:460
  45.9 15.3 %collective-permute-start.4 = (bf16[4,16,32,128]{3,2,1,0:T(8,128)(2,1)S(1)}, bf16[4,16,32,128]{3,2,1,0:T(8,128)(2,1)}, u32[]{:S(2)}, u32[]{:S(2)}) collective-permute-start(bf16[4,16,32,128]{3,2,1,0:T(8,128)(2,1)S(1)} %pad_maximum_fusion.1.gu_0), channel_id=1, source_target_pairs={{0,128},{64,192},{128,0},{192,64},{16,144},{80,208},{144,16},{208,... | collective-permute-start | bytes 1572872 | tf_op jit(solution)/shard_map/ppermute | solution.py:460
  48.7 12.6 %collective-permute-start.5 = (bf16[4,16,32,128]{3,2,1,0:T(8,128)(2,1)S(1)}, bf16[4,16,32,128]{3,2,1,0:T(8,128)(2,1)}, u32[]{:S(2)}, u32[]{:S(2)}) collective-permute-start(bf16[4,16,32,128]{3,2,1,0:T(8,128)(2,1)S(1)} %pad_maximum_fusion.1.gu_0), channel_id=1, source_target_pairs={{0,192},{64,0},{128,64},{192,128},{16,208},{80,16},{144,80},{208,1... | collective-permute-start | bytes 1572872 | tf_op jit(solution)/shard_map/ppermute | solution.py:460
  74.9 12.5 %copy-start.2 = (bf16[4,24,32,128]{3,2,1,0:T(8,128)(2,1)}, bf16[4,24,32,128]{3,2,1,0:T(8,128)(2,1)S(1)}, u32[]{:S(2)}) copy-start(bf16[4,24,32,128]{3,2,1,0:T(8,128)(2,1)S(1)} %get-tuple-element.44) | copy-start | bytes 2359300
  74.9 12.5 %collective-permute-start.6 = (bf16[4,24,32,128]{3,2,1,0:T(8,128)(2,1)S(1)}, bf16[4,24,32,128]{3,2,1,0:T(8,128)(2,1)S(1)}, u32[]{:S(2)}, u32[]{:S(2)}) collective-permute-start(bf16[4,24,32,128]{3,2,1,0:T(8,128)(2,1)S(1)} %get-tuple-element.35), channel_id=1, source_target_pairs={{0,64},{64,128},{128,192},{192,0},{16,80},{80,144},{144,208},{208,... | collective-permute-start | bytes 2359304 | tf_op jit(solution)/shard_map/ppermute | solution.py:460
  76.2 20.8 %collective-permute-start.7 = (bf16[4,24,32,128]{3,2,1,0:T(8,128)(2,1)S(1)}, bf16[4,24,32,128]{3,2,1,0:T(8,128)(2,1)S(1)}, u32[]{:S(2)}, u32[]{:S(2)}) collective-permute-start(bf16[4,24,32,128]{3,2,1,0:T(8,128)(2,1)S(1)} %get-tuple-element.36), channel_id=1, source_target_pairs={{0,128},{64,192},{128,0},{192,64},{16,144},{80,208},{144,16},{208,... | collective-permute-start | bytes 2359304 | tf_op jit(solution)/shard_map/ppermute | solution.py:460
  78.9 18.1 %collective-permute-start.8 = (bf16[4,24,32,128]{3,2,1,0:T(8,128)(2,1)S(1)}, bf16[4,24,32,128]{3,2,1,0:T(8,128)(2,1)S(1)}, u32[]{:S(2)}, u32[]{:S(2)}) collective-permute-start(bf16[4,24,32,128]{3,2,1,0:T(8,128)(2,1)S(1)} %get-tuple-element.37), channel_id=1, source_target_pairs={{0,192},{64,0},{128,64},{192,128},{16,208},{80,16},{144,80},{208,1... | collective-permute-start | bytes 2359304 | tf_op jit(solution)/shard_map/ppermute | solution.py:460
  87.4 9.6 %copy-start.5 = (bf16[4,24,32,128]{3,2,1,0:T(8,128)(2,1)}, bf16[4,24,32,128]{3,2,1,0:T(8,128)(2,1)S(1)}, u32[]{:S(2)}) copy-start(bf16[4,24,32,128]{3,2,1,0:T(8,128)(2,1)S(1)} %collective-permute-done.6) | copy-start | bytes 2359300
  97.0 0.9 copy-start.7
  97.0 1.1 copy-start.9
  98.1 1.1 copy-start.3
  98.1 1.4 copy-start.6
  98.1 1.6 copy-start.8
  101.3 6.4 %collective-permute-start.10 = (bf16[24,32,128]{2,1,0:T(8,128)(2,1)S(1)}, bf16[24,32,128]{2,1,0:T(8,128)(2,1)S(1)}, u32[]{:S(2)}, u32[]{:S(2)}) collective-permute-start(bf16[24,32,128]{2,1,0:T(8,128)(2,1)S(1)} %get-tuple-element.53), channel_id=1, source_target_pairs={{0,32},{16,48},{32,0},{48,16},{64,96},{80,112},{96,64},{112,80},{1... | collective-permute-start | bytes 589832 | tf_op jit(solution)/shard_map/ppermute | solution.py:460
  103.8 5.8 %collective-permute-start.11 = (bf16[24,32,128]{2,1,0:T(8,128)(2,1)S(1)}, bf16[24,32,128]{2,1,0:T(8,128)(2,1)S(1)}, u32[]{:S(2)}, u32[]{:S(2)}) collective-permute-start(bf16[24,32,128]{2,1,0:T(8,128)(2,1)S(1)} %get-tuple-element.52), channel_id=1, source_target_pairs={{0,48},{16,0},{32,16},{48,32},{64,112},{80,64},{96,80},{112,96},{1... | collective-permute-start | bytes 589832 | tf_op jit(solution)/shard_map/ppermute | solution.py:460
  104.7 5.7 %collective-permute-start.9 = (bf16[24,32,128]{2,1,0:T(8,128)(2,1)S(1)}, bf16[24,32,128]{2,1,0:T(8,128)(2,1)S(1)}, u32[]{:S(2)}, u32[]{:S(2)}) collective-permute-start(bf16[24,32,128]{2,1,0:T(8,128)(2,1)S(1)} %get-tuple-element.51), channel_id=1, source_target_pairs={{0,16},{16,32},{32,48},{48,0},{64,80},{80,96},{96,112},{112,64},{1... | collective-permute-start | bytes 589832 | tf_op jit(solution)/shard_map/ppermute | solution.py:460
  111.2 17.3 %all-to-all-start.1 = ((bf16[16,32,128]{2,1,0:T(8,128)(2,1)}), bf16[16,32,128]{2,1,0:T(8,128)(2,1)S(1)}, u32[]{:S(2)}, u32[]{:S(2)}) async-start(bf16[16,32,128]{2,1,0:T(8,128)(2,1)} %fusion.3), calls=%async_computation.2 | async-start | bytes 262144 | tf_op jit(solution)/shard_map/all_to_all | solution.py:576
  128.6 6.1 %collective-permute-start.12 = (bf16[24,32,128]{2,1,0:T(8,128)(2,1)S(1)}, bf16[24,32,128]{2,1,0:T(8,128)(2,1)S(1)}, u32[]{:S(2)}, u32[]{:S(2)}) collective-permute-start(bf16[24,32,128]{2,1,0:T(8,128)(2,1)S(1)} %get-tuple-element.55), channel_id=1, source_target_pairs={{0,16},{16,32},{32,48},{48,0},{64,80},{80,96},{96,112},{112,64},{1... | collective-permute-start | bytes 589832 | tf_op jit(solution)/shard_map/ppermute | solution.py:460
  130.1 6.9 %collective-permute-start.13 = (bf16[24,32,128]{2,1,0:T(8,128)(2,1)S(1)}, bf16[24,32,128]{2,1,0:T(8,128)(2,1)S(1)}, u32[]{:S(2)}, u32[]{:S(2)}) collective-permute-start(bf16[24,32,128]{2,1,0:T(8,128)(2,1)S(1)} %get-tuple-element.55), channel_id=1, source_target_pairs={{0,32},{16,48},{32,0},{48,16},{64,96},{80,112},{96,64},{112,80},{1... | collective-permute-start | bytes 589832 | tf_op jit(solution)/shard_map/ppermute | solution.py:460
  131.8 5.6 %collective-permute-start.14 = (bf16[24,32,128]{2,1,0:T(8,128)(2,1)S(1)}, bf16[24,32,128]{2,1,0:T(8,128)(2,1)S(1)}, u32[]{:S(2)}, u32[]{:S(2)}) collective-permute-start(bf16[24,32,128]{2,1,0:T(8,128)(2,1)S(1)} %get-tuple-element.55), channel_id=1, source_target_pairs={{0,48},{16,0},{32,16},{48,32},{64,112},{80,64},{96,80},{112,96},{1... | collective-permute-start | bytes 589832 | tf_op jit(solution)/shard_map/ppermute | solution.py:460
  137.5 20.8 %collective-permute-start.15 = (bf16[4,24,32,128]{3,2,1,0:T(8,128)(2,1)S(1)}, bf16[4,24,32,128]{3,2,1,0:T(8,128)(2,1)S(1)}, u32[]{:S(2)}, u32[]{:S(2)}) collective-permute-start(bf16[4,24,32,128]{3,2,1,0:T(8,128)(2,1)S(1)} %pad_maximum_fusion.full_0), channel_id=1, source_target_pairs={{0,64},{64,128},{128,192},{192,0},{16,80},{80,144},{144,208},{208,... | collective-permute-start | bytes 2359304 | tf_op jit(solution)/shard_map/ppermute | solution.py:460
  137.6 20.8 %collective-permute-start.16 = (bf16[4,24,32,128]{3,2,1,0:T(8,128)(2,1)S(1)}, bf16[4,24,32,128]{3,2,1,0:T(8,128)(2,1)S(1)}, u32[]{:S(2)}, u32[]{:S(2)}) collective-permute-start(bf16[4,24,32,128]{3,2,1,0:T(8,128)(2,1)S(1)} %pad_maximum_fusion.full_0), channel_id=1, source_target_pairs={{0,128},{64,192},{128,0},{192,64},{16,144},{80,208},{144,16},{208,... | collective-permute-start | bytes 2359304 | tf_op jit(solution)/shard_map/ppermute | solution.py:460
  139.7 19.4 %collective-permute-start.17 = (bf16[4,24,32,128]{3,2,1,0:T(8,128)(2,1)S(1)}, bf16[4,24,32,128]{3,2,1,0:T(8,128)(2,1)S(1)}, u32[]{:S(2)}, u32[]{:S(2)}) collective-permute-start(bf16[4,24,32,128]{3,2,1,0:T(8,128)(2,1)S(1)} %pad_maximum_fusion.full_0), channel_id=1, source_target_pairs={{0,192},{64,0},{128,64},{192,128},{16,208},{80,16},{144,80},{208,1... | collective-permute-start | bytes 2359304 | tf_op jit(solution)/shard_map/ppermute | solution.py:460
Sparse Core Ops, SparseCore 0:
  10.8 51.5 all-gather.2
  98.3 60.6 reduce-scatter.1

commit v4 on v3

--- a/solution.py
+++ b/solution.py
@@ -465,9 +465,7 @@
     return [row] + [shift(row, False, k) for k in range(1, SIDE)]
 
 
-def from_replicas(parts, second):
-    got = parts
-    rows = sum(part.astype(F32) for part in got).astype(BF)
+def from_replicas(rows, second):
     ahead = [
         lax.dynamic_index_in_dim(rows, (second + k) % SIDE, 0, keepdims=False)
         for k in range(SIDE)
@@ -566,13 +564,14 @@
     grads, hidden_split, pre = layer(place, meta, dmeta, act, down, gu)
     grads = [grads[0]] + [shift(grads[k], False, k) for k in range(1, SIDE)]
     partials = output_part(place, meta, dmeta, down_t, hidden_split, pre, gu)
-    *grads, partials = lax.optimization_barrier((*grads, partials))
+    rows = sum(part.astype(F32) for part in grads).astype(BF)
+    rows, partials = lax.optimization_barrier((rows, partials))
 
     summed = lax.psum_scatter(
         partials.reshape(GROUPS * 2 * width, 128), "mp", scatter_dimension=0, tiled=True
     )
 
-    got_gu, got_down = from_replicas(grads, part % SIDE)
+    got_gu, got_down = from_replicas(rows, part % SIDE)
     back = lax.all_to_all(got_gu, "mp", 0, 0, tiled=True)
     piece = jnp.concatenate([jnp.where(my_live, back, 0), got_down], axis=0)
     flat = (GROUPS * DEPTH * HALF, 128)

time: 172 us -> 171 us (level)
  local copies, waits for them, and re-layouts: 5.95 us -> 3.3 us
    unnamed x34 -> x20, local copies, waits for them, and re-layouts: 3.63 us -> 0.98 us
    reduce_scatter x1, waiting for transfers between devices: 0.02 us -> 1.94 us  [per_device(): lax.psum_scatter(partials.reshape(GROUPS * 2 * width, 128), 'mp', scatter...]
  transfers between devices with their start and end apart: 22 -> 22, of which waited for: 14 -> 15; matrix products, arithmetic and copies ran while one was open for 5% -> 4% of each run, Pallas kernels for 8% -> 8%
where the time goes in v4:
time: 171 us; the launch traced here: 168 us
  waiting for transfers between devices  70.9 us (41%)
  starting transfers between devices  44.8 us (26%)
  Pallas kernels  27.4 us (16%)
  between operations  14.6 us (9%)
  other arithmetic  5.63 us (3%)
  local copies, waits for them, and re-layouts  3.3 us (2%)
    ppermute x18, waiting for transfers between devices, shift(): return lax.ppermute(value, ('dp', 'mp'), pairs)  48.3 us
    ppermute x18, starting transfers between devices, shift(): return lax.ppermute(value, ('dp', 'mp'), pairs)  27.2 us
    pallas_call x1, Pallas kernels, layer(): pl.pallas_call(layer_kernel, out_shape=(piece,) * SIDE + (jax.ShapeDtypeS...  12.4 us
    all_to_all x1, starting transfers between devices, per_device(): lax.all_to_all(jnp.concatenate([mine, notes], axis=1), 'mp', 0, 0, tiled=...  9.98 us
    all_to_all x1, waiting for transfers between devices, per_device(): lax.all_to_all(jnp.concatenate([mine, notes], axis=1), 'mp', 0, 0, tiled=...  9.85 us
    all_to_all x1, waiting for transfers between devices, per_device(): back = lax.all_to_all(got_gu, 'mp', 0, 0, tiled=True)  9.68 us
    all_to_all x1, starting transfers between devices, per_device(): back = lax.all_to_all(got_gu, 'mp', 0, 0, tiled=True)  7.47 us
    pallas_call x1, Pallas kernels, output_part(): pl.pallas_call(output_kernel, out_shape=jax.ShapeDtypeStruct((GROUPS, 2,...  7.41 us
  transfers between devices with their start and end apart: 22, of which 15 were waited for; matrix products, arithmetic and copies ran while one was open for 4% of the time, Pallas kernels for 8%

profile of v4, /device:TPU:1, one launch (start us, length us, event | category | flops | bytes accessed | tf_op | source)
XLA Modules:
  0.0 168.2 jit_solution(7504517388585139357)
XLA Ops:
  7.3 0.8 copy-done
  8.1 0.4 convolution_convert_fusion.1
  8.4 0.1 copy.37
  8.6 1.3 convolution_convert_fusion
  9.9 0.8 pad_maximum_fusion.2
  11.1 0.1 copy.44
  11.2 0.1 copy.45
  11.5 0.1 copy.46
  11.6 0.1 copy.47
  11.7 0.1 fusion.17
  11.8 1.1 fusion.5
  12.9 0.7 pad_maximum_fusion.4
  13.6 10.0 %all-to-all-start = ((bf16[16,40,128]{2,1,0:T(8,128)(2,1)}), bf16[16,40,128]{2,1,0:T(8,128)(2,1)S(1)}, u32[]{:S(2)}, u32[]{:S(2)}) async-start(bf16[16,40,128]{2,1,0:T(8,128)(2,1)} %pad_maximum_fusion.4), calls=%async_computation | async-start | bytes 327680 | tf_op jit(solution)/shard_map/all_to_all | solution.py:541
  23.8 0.1 lt.117
  23.9 0.2 broadcast_select_fusion.down
  24.1 9.8 %all-to-all-done = bf16[16,40,128]{2,1,0:T(8,128)(2,1)S(1)} async-done(((bf16[16,40,128]{2,1,0:T(8,128)(2,1)}), bf16[16,40,128]{2,1,0:T(8,128)(2,1)S(1)}, u32[]{:S(2)}, u32[]{:S(2)}) %all-to-all-start) | async-done | bytes 163872 | tf_op jit(solution)/shard_map/all_to_all | solution.py:541
  34.0 0.7 slice_bitcast_fusion
  34.7 1.2 collective-permute-start
  35.9 2.5 %collective-permute-start.1 = (bf16[16,32,128]{2,1,0:T(8,128)(2,1)}, bf16[16,32,128]{2,1,0:T(8,128)(2,1)}, u32[]{:S(2)}, u32[]{:S(2)}) collective-permute-start(bf16[16,32,128]{2,1,0:T(8,128)(2,1)} %get-tuple-element.51), channel_id=1, source_target_pairs={{0,32},{16,48},{32,0},{48,16},{64,96},{80,112},{96,64},{112,80},{1... | collective-permute-start | bytes 393224 | tf_op jit(solution)/shard_map/ppermute | solution.py:460
  38.4 1.2 collective-permute-start.2
  39.5 0.1 squeeze.29
  39.7 0.1 sub.120
  39.8 0.1 sub.118
  39.9 0.1 reshape.326
  40.0 3.3 %turn_kernel.1.down_t = bf16[128,64,64]{2,1,0:T(8,128)(2,1)S(1)} custom-call(bf16[128,32,128]{2,1,0:T(8,128)(2,1)S(1)} %broadcast_select_fusion.down), custom_call_target="tpu_custom_call" | custom-call | flops 67108864 | bytes 4194304 | tf_op jit(solution)/shard_map/turn_kernel/pallas_call | solution.py:339
  43.4 1.2 pad_maximum_fusion.1.gu_0
  44.5 1.4 collective-permute-start.3
  45.9 2.8 %collective-permute-start.4 = (bf16[4,16,32,128]{3,2,1,0:T(8,128)(2,1)S(1)}, bf16[4,16,32,128]{3,2,1,0:T(8,128)(2,1)}, u32[]{:S(2)}, u32[]{:S(2)}) collective-permute-start(bf16[4,16,32,128]{3,2,1,0:T(8,128)(2,1)S(1)} %pad_maximum_fusion.1.gu_0), channel_id=1, source_target_pairs={{0,128},{64,192},{128,0},{192,64},{16,144},{80,208},{144,16},{208,... | collective-permute-start | bytes 1572872 | tf_op jit(solution)/shard_map/ppermute | solution.py:460
  48.7 1.0 collective-permute-start.5
  50.0 4.5 %collective-permute-done.3.gu_1 = bf16[4,16,32,128]{3,2,1,0:T(8,128)(2,1)S(1)} collective-permute-done((bf16[4,16,32,128]{3,2,1,0:T(8,128)(2,1)S(1)}, bf16[4,16,32,128]{3,2,1,0:T(8,128)(2,1)S(1)}, u32[]{:S(2)}, u32[]{:S(2)}) %collective-permute-start.3) | collective-permute-done | bytes 524320 | tf_op jit(solution)/shard_map/ppermute | solution.py:460
  54.5 6.8 %collective-permute-done.4.gu_2 = bf16[4,16,32,128]{3,2,1,0:T(8,128)(2,1)} collective-permute-done((bf16[4,16,32,128]{3,2,1,0:T(8,128)(2,1)S(1)}, bf16[4,16,32,128]{3,2,1,0:T(8,128)(2,1)}, u32[]{:S(2)}, u32[]{:S(2)}) %collective-permute-start.4) | collective-permute-done | bytes 524320 | tf_op jit(solution)/shard_map/ppermute | solution.py:460
  61.3 1.1 all-gather.3.cloned.1.call-done
  62.4 12.4 %layer_kernel.1 = (bf16[4,24,32,128]{3,2,1,0:T(8,128)(2,1)S(1)}, bf16[4,24,32,128]{3,2,1,0:T(8,128)(2,1)S(1)}, bf16[4,24,32,128]{3,2,1,0:T(8,128)(2,1)S(1)}, bf1...) custom-call(s32[2]{0:T(128)S(1)} %pad_add_fusion.1.place, ...), custom_call_target="tpu_custom_call" | custom-call | flops 536870912 | bytes 8388608 | tf_op jit(solution)/shard_map/layer_kernel/pallas_call | solution.py:354
  74.8 1.4 collective-permute-start.6
  76.2 2.7 %collective-permute-start.7 = (bf16[4,24,32,128]{3,2,1,0:T(8,128)(2,1)S(1)}, bf16[4,24,32,128]{3,2,1,0:T(8,128)(2,1)S(1)}, u32[]{:S(2)}, u32[]{:S(2)}) collective-permute-start(bf16[4,24,32,128]{3,2,1,0:T(8,128)(2,1)S(1)} %get-tuple-element.33), channel_id=1, source_target_pairs={{0,128},{64,192},{128,0},{192,64},{16,144},{80,208},{144,16},{208,... | collective-permute-start | bytes 2359304 | tf_op jit(solution)/shard_map/ppermute | solution.py:460
  78.9 1.0 collective-permute-start.8
  79.9 7.4 %output_kernel.1 = bf16[16,2,8,64,128]{4,3,2,1,0:T(8,128)(2,1)} custom-call(s32[2]{0:T(128)S(1)} %pad_add_fusion.1.place, s32[16,32]{1,0:T(8,128)S(1)} %copy.50.meta, s32[3,128]{1,0:T(4,128)S(1)} %pad_add_fusion.dmeta, bf16[128,64,64]{2,1,0:T(8,128)(2,1)S(1)} %turn_kernel.1.down_t, bf16[14,64,128]{2,1,0:T(8,128)(2,1)S(1)} %get-tuple-element.36.hidden_split, ...), custom_call_target="tpu_custom_call" | custom-call | flops 268435456 | bytes 8388608 | tf_op jit(solution)/shard_map/output_kernel/pallas_call | solution.py:383
  87.4 9.6 %collective-permute-done.7 = bf16[4,24,32,128]{3,2,1,0:T(8,128)(2,1)S(1)} collective-permute-done((bf16[4,24,32,128]{3,2,1,0:T(8,128)(2,1)S(1)}, bf16[4,24,32,128]{3,2,1,0:T(8,128)(2,1)S(1)}, u32[]{:S(2)}, u32[]{:S(2)}) %collective-permute-start.7) | collective-permute-done | bytes 786464 | tf_op jit(solution)/shard_map/ppermute | solution.py:460
  97.0 0.4 add_convert_fusion
  97.5 2.5 %collective-permute-start.10 = (bf16[24,32,128]{2,1,0:T(8,128)(2,1)S(1)}, bf16[24,32,128]{2,1,0:T(8,128)(2,1)S(1)}, u32[]{:S(2)}, u32[]{:S(2)}) collective-permute-start(bf16[24,32,128]{2,1,0:T(8,128)(2,1)S(1)} %get-tuple-element.47), channel_id=1, source_target_pairs={{0,32},{16,48},{32,0},{48,16},{64,96},{80,112},{96,64},{112,80},{1... | collective-permute-start | bytes 589832 | tf_op jit(solution)/shard_map/ppermute | solution.py:460
  100.0 0.9 collective-permute-start.11
  100.9 0.6 collective-permute-start.9
  101.5 2.4 %collective-permute-done.10 = bf16[24,32,128]{2,1,0:T(8,128)(2,1)S(1)} collective-permute-done((bf16[24,32,128]{2,1,0:T(8,128)(2,1)S(1)}, bf16[24,32,128]{2,1,0:T(8,128)(2,1)S(1)}, u32[]{:S(2)}, u32[]{:S(2)}) %collective-permute-start.10) | collective-permute-done | bytes 196640 | tf_op jit(solution)/shard_map/ppermute | solution.py:460
  103.9 1.8 %collective-permute-done.11 = bf16[24,32,128]{2,1,0:T(8,128)(2,1)S(1)} collective-permute-done((bf16[24,32,128]{2,1,0:T(8,128)(2,1)S(1)}, bf16[24,32,128]{2,1,0:T(8,128)(2,1)S(1)}, u32[]{:S(2)}, u32[]{:S(2)}) %collective-permute-start.11) | collective-permute-done | bytes 196640 | tf_op jit(solution)/shard_map/ppermute | solution.py:460
  105.8 0.9 collective-permute-done.9
  106.6 0.7 fusion.3
  107.4 7.5 %all-to-all-start.1 = ((bf16[16,32,128]{2,1,0:T(8,128)(2,1)}), bf16[16,32,128]{2,1,0:T(8,128)(2,1)S(1)}, u32[]{:S(2)}, u32[]{:S(2)}) async-start(bf16[16,32,128]{2,1,0:T(8,128)(2,1)} %fusion.3), calls=%async_computation.2 | async-start | bytes 262144 | tf_op jit(solution)/shard_map/all_to_all | solution.py:575
  114.9 9.7 %all-to-all-done.1 = bf16[16,32,128]{2,1,0:T(8,128)(2,1)S(1)} async-done(((bf16[16,32,128]{2,1,0:T(8,128)(2,1)}), bf16[16,32,128]{2,1,0:T(8,128)(2,1)S(1)}, u32[]{:S(2)}, u32[]{:S(2)}) %all-to-all-start.1) | async-done | bytes 131104 | tf_op jit(solution)/shard_map/all_to_all | solution.py:575
  124.5 0.1 broadcast_select_fusion.1
  124.7 1.8 %collective-permute-start.12 = (bf16[24,32,128]{2,1,0:T(8,128)(2,1)S(1)}, bf16[24,32,128]{2,1,0:T(8,128)(2,1)S(1)}, u32[]{:S(2)}, u32[]{:S(2)}) collective-permute-start(bf16[24,32,128]{2,1,0:T(8,128)(2,1)S(1)} %get-tuple-element.49), channel_id=1, source_target_pairs={{0,16},{16,32},{32,48},{48,0},{64,80},{80,96},{96,112},{112,64},{1... | collective-permute-start | bytes 589832 | tf_op jit(solution)/shard_map/ppermute | solution.py:460
  126.4 1.7 %collective-permute-start.13 = (bf16[24,32,128]{2,1,0:T(8,128)(2,1)S(1)}, bf16[24,32,128]{2,1,0:T(8,128)(2,1)S(1)}, u32[]{:S(2)}, u32[]{:S(2)}) collective-permute-start(bf16[24,32,128]{2,1,0:T(8,128)(2,1)S(1)} %get-tuple-element.49), channel_id=1, source_target_pairs={{0,32},{16,48},{32,0},{48,16},{64,96},{80,112},{96,64},{112,80},{1... | collective-permute-start | bytes 589832 | tf_op jit(solution)/shard_map/ppermute | solution.py:460
  128.2 1.3 collective-permute-start.14
  129.5 1.4 collective-permute-done.12
  130.9 2.4 %collective-permute-done.13 = bf16[24,32,128]{2,1,0:T(8,128)(2,1)S(1)} collective-permute-done((bf16[24,32,128]{2,1,0:T(8,128)(2,1)S(1)}, bf16[24,32,128]{2,1,0:T(8,128)(2,1)S(1)}, u32[]{:S(2)}, u32[]{:S(2)}) %collective-permute-start.13) | collective-permute-done | bytes 196640 | tf_op jit(solution)/shard_map/ppermute | solution.py:460
  133.3 0.1 collective-permute-done.14
  133.5 0.1 pad_maximum_fusion.full_0
  133.6 0.1 collective-permute-start.15
  133.7 2.3 %collective-permute-start.16 = (bf16[4,24,32,128]{3,2,1,0:T(8,128)(2,1)S(1)}, bf16[4,24,32,128]{3,2,1,0:T(8,128)(2,1)S(1)}, u32[]{:S(2)}, u32[]{:S(2)}) collective-permute-start(bf16[4,24,32,128]{3,2,1,0:T(8,128)(2,1)S(1)} %pad_maximum_fusion.full_0), channel_id=1, source_target_pairs={{0,128},{64,192},{128,0},{192,64},{16,144},{80,208},{144,16},{208,... | collective-permute-start | bytes 2359304 | tf_op jit(solution)/shard_map/ppermute | solution.py:460
  135.9 1.0 collective-permute-start.17
  137.0 17.5 %collective-permute-done.15.full_1 = bf16[4,24,32,128]{3,2,1,0:T(8,128)(2,1)S(1)} collective-permute-done((bf16[4,24,32,128]{3,2,1,0:T(8,128)(2,1)S(1)}, bf16[4,24,32,128]{3,2,1,0:T(8,128)(2,1)S(1)}, u32[]{:S(2)}, u32[]{:S(2)}) %collective-permute-start.15) | collective-permute-done | bytes 786464 | tf_op jit(solution)/shard_map/ppermute | solution.py:460
  154.4 0.7 collective-permute-done.17.full_3
  155.1 2.5 %place_kernel.1 = (bf16[16,8,32,128]{3,2,1,0:T(8,128)(2,1)}, bf16[16,8,32,128]{3,2,1,0:T(8,128)(2,1)}, bf16[16,8,32,128]{3,2,1,0:T(8,128)(2,1)}) custom-call(s32[2]{0:T(128)S(1)} %pad_add_fusion.1.place, bf16[4,24,32,128]{3,2,1,0:T(8,128)(2,1)S(1)} %pad_maximum_fusion.full_0, bf16[4,24,32,128]{3,2,1,0:T(8,128)(2,1)S(1)} %collective-permute-done.15.full_1, ...), custom_call_target="tpu_custom_call" | custom-call | bytes 4194304 | tf_op jit(solution)/shard_map/place_kernel/pallas_call | solution.py:404
  157.6 1.9 %reduce-scatter.2.cloned.1.call-done.summed = bf16[1024,128]{1,0:T(8,128)(2,1)} async-done(((bf16[16384,128]{1,0:T(8,128)(2,1)}), bf16[1024,128]{1,0:T(8,128)(2,1)}) %reduce-scatter.2.cloned.1.call-update) | async-done | bytes 262160 | tf_op jit(solution)/shard_map/reduce_scatter | solution.py:570
  159.6 1.8 %turn_back_kernel.1 = (bf16[128,512]{1,0:T(8,128)(2,1)}, bf16[128,512]{1,0:T(8,128)(2,1)}) custom-call(bf16[1024,128]{1,0:T(8,128)(2,1)} %reduce-scatter.2.cloned.1.call-done.summed), custom_call_target="tpu_custom_call" | custom-call | bytes 524288 | tf_op jit(solution)/shard_map/turn_back_kernel/pallas_call | solution.py:419
  (57 shorter events, 1.3 us)
Async XLA Ops:
  7.2 0.9 copy-start
  7.2 3.6 %copy-start.3 = (s32[128,2]{0,1:T(2,128)S(1)}, s32[128,2]{0,1:T(2,128)}, u32[]{:S(2)}) copy-start(s32[128,2]{0,1:T(2,128)} %param.13) | copy-start | bytes 3076
  7.2 3.8 %copy-start.4 = (s32[128,2]{0,1:T(2,128)S(1)}, s32[128,2]{0,1:T(2,128)}, u32[]{:S(2)}) copy-start(s32[128,2]{0,1:T(2,128)} %param.16) | copy-start | bytes 3076
  7.2 4.6 %copy-start.7 = (s32[16]{0:T(128)S(1)}, s32[16]{0:T(128)}, u32[]{:S(2)}) copy-start(s32[16]{0:T(128)} %param.14) | copy-start | bytes 196
  7.2 4.6 %copy-start.6 = (s32[16]{0:T(128)S(1)}, s32[16]{0:T(128)}, u32[]{:S(2)}) copy-start(s32[16]{0:T(128)} %param.17) | copy-start | bytes 196
  7.2 55.2 %all-gather.3.cloned.1.call-start = ((), (), s32[]{:S(2)}) async-start(), calls=%async_computation.4 | async-start | bytes 6684672 | tf_op jit(solution)/shard_map/all_gather | solution.py:513
  8.6 15.0 %copy-start.5 = (s32[128,2]{0,1:T(2,128)S(1)}, s32[128,2]{0,1:T(2,128)}, u32[]{:S(2)}) copy-start(s32[128,2]{0,1:T(2,128)} %param.19) | copy-start | bytes 3076
  8.6 15.1 %copy-start.8 = (s32[16]{0:T(128)S(1)}, s32[16]{0:T(128)}, u32[]{:S(2)}) copy-start(s32[16]{0:T(128)} %param.20) | copy-start | bytes 196
  8.6 15.3 %copy-start.2 = (bf16[4096,128]{1,0:T(8,128)(2,1)S(1)}, bf16[4096,128]{1,0:T(8,128)(2,1)}, u32[]{:S(2)}) copy-start(bf16[4096,128]{1,0:T(8,128)(2,1)} %param.18) | copy-start | bytes 3145732
  13.6 20.4 %all-to-all-start = ((bf16[16,40,128]{2,1,0:T(8,128)(2,1)}), bf16[16,40,128]{2,1,0:T(8,128)(2,1)S(1)}, u32[]{:S(2)}, u32[]{:S(2)}) async-start(bf16[16,40,128]{2,1,0:T(8,128)(2,1)} %pad_maximum_fusion.4), calls=%async_computation | async-start | bytes 327680 | tf_op jit(solution)/shard_map/all_to_all | solution.py:541
  23.5 136.0 %reduce-scatter.2.cloned.1.call-start = ((), (), s32[]{:S(2)}) async-start(), calls=%async_computation.3 | async-start | bytes 4456448 | tf_op jit(solution)/shard_map/reduce_scatter | solution.py:570
  24.1 19.2 %copy-start.1 = (bf16[128,32,128]{2,1,0:T(8,128)(2,1)}, bf16[128,32,128]{2,1,0:T(8,128)(2,1)S(1)}, u32[]{:S(2)}) copy-start(bf16[128,32,128]{2,1,0:T(8,128)(2,1)S(1)} %broadcast_select_fusion.down) | copy-start | bytes 3145732
  34.7 8.7 %collective-permute-start = (bf16[16,32,128]{2,1,0:T(8,128)(2,1)}, bf16[16,32,128]{2,1,0:T(8,128)(2,1)}, u32[]{:S(2)}, u32[]{:S(2)}) collective-permute-start(bf16[16,32,128]{2,1,0:T(8,128)(2,1)} %get-tuple-element.51), channel_id=1, source_target_pairs={{0,16},{16,32},{32,48},{48,0},{64,80},{80,96},{96,112},{112,64},{1... | collective-permute-start | bytes 393224 | tf_op jit(solution)/shard_map/ppermute | solution.py:460
  35.9 7.5 %collective-permute-start.1 = (bf16[16,32,128]{2,1,0:T(8,128)(2,1)}, bf16[16,32,128]{2,1,0:T(8,128)(2,1)}, u32[]{:S(2)}, u32[]{:S(2)}) collective-permute-start(bf16[16,32,128]{2,1,0:T(8,128)(2,1)} %get-tuple-element.51), channel_id=1, source_target_pairs={{0,32},{16,48},{32,0},{48,16},{64,96},{80,112},{96,64},{112,80},{1... | collective-permute-start | bytes 393224 | tf_op jit(solution)/shard_map/ppermute | solution.py:460
  38.4 5.0 %collective-permute-start.2 = (bf16[16,32,128]{2,1,0:T(8,128)(2,1)}, bf16[16,32,128]{2,1,0:T(8,128)(2,1)}, u32[]{:S(2)}, u32[]{:S(2)}) collective-permute-start(bf16[16,32,128]{2,1,0:T(8,128)(2,1)} %get-tuple-element.51), channel_id=1, source_target_pairs={{0,48},{16,0},{32,16},{48,32},{64,112},{80,64},{96,80},{112,96},{1... | collective-permute-start | bytes 393224 | tf_op jit(solution)/shard_map/ppermute | solution.py:460
  44.5 9.9 %collective-permute-start.3 = (bf16[4,16,32,128]{3,2,1,0:T(8,128)(2,1)S(1)}, bf16[4,16,32,128]{3,2,1,0:T(8,128)(2,1)S(1)}, u32[]{:S(2)}, u32[]{:S(2)}) collective-permute-start(bf16[4,16,32,128]{3,2,1,0:T(8,128)(2,1)S(1)} %pad_maximum_fusion.1.gu_0), channel_id=1, source_target_pairs={{0,64},{64,128},{128,192},{192,0},{16,80},{80,144},{144,208},{208,... | collective-permute-start | bytes 1572872 | tf_op jit(solution)/shard_map/ppermute | solution.py:460
  45.9 15.3 %collective-permute-start.4 = (bf16[4,16,32,128]{3,2,1,0:T(8,128)(2,1)S(1)}, bf16[4,16,32,128]{3,2,1,0:T(8,128)(2,1)}, u32[]{:S(2)}, u32[]{:S(2)}) collective-permute-start(bf16[4,16,32,128]{3,2,1,0:T(8,128)(2,1)S(1)} %pad_maximum_fusion.1.gu_0), channel_id=1, source_target_pairs={{0,128},{64,192},{128,0},{192,64},{16,144},{80,208},{144,16},{208,... | collective-permute-start | bytes 1572872 | tf_op jit(solution)/shard_map/ppermute | solution.py:460
  48.7 12.6 %collective-permute-start.5 = (bf16[4,16,32,128]{3,2,1,0:T(8,128)(2,1)S(1)}, bf16[4,16,32,128]{3,2,1,0:T(8,128)(2,1)}, u32[]{:S(2)}, u32[]{:S(2)}) collective-permute-start(bf16[4,16,32,128]{3,2,1,0:T(8,128)(2,1)S(1)} %pad_maximum_fusion.1.gu_0), channel_id=1, source_target_pairs={{0,192},{64,0},{128,64},{192,128},{16,208},{80,16},{144,80},{208,1... | collective-permute-start | bytes 1572872 | tf_op jit(solution)/shard_map/ppermute | solution.py:460
  74.8 12.5 %collective-permute-start.6 = (bf16[4,24,32,128]{3,2,1,0:T(8,128)(2,1)S(1)}, bf16[4,24,32,128]{3,2,1,0:T(8,128)(2,1)S(1)}, u32[]{:S(2)}, u32[]{:S(2)}) collective-permute-start(bf16[4,24,32,128]{3,2,1,0:T(8,128)(2,1)S(1)} %get-tuple-element.32), channel_id=1, source_target_pairs={{0,64},{64,128},{128,192},{192,0},{16,80},{80,144},{144,208},{208,... | collective-permute-start | bytes 2359304 | tf_op jit(solution)/shard_map/ppermute | solution.py:460
  76.2 20.8 %collective-permute-start.7 = (bf16[4,24,32,128]{3,2,1,0:T(8,128)(2,1)S(1)}, bf16[4,24,32,128]{3,2,1,0:T(8,128)(2,1)S(1)}, u32[]{:S(2)}, u32[]{:S(2)}) collective-permute-start(bf16[4,24,32,128]{3,2,1,0:T(8,128)(2,1)S(1)} %get-tuple-element.33), channel_id=1, source_target_pairs={{0,128},{64,192},{128,0},{192,64},{16,144},{80,208},{144,16},{208,... | collective-permute-start | bytes 2359304 | tf_op jit(solution)/shard_map/ppermute | solution.py:460
  78.9 18.1 %collective-permute-start.8 = (bf16[4,24,32,128]{3,2,1,0:T(8,128)(2,1)S(1)}, bf16[4,24,32,128]{3,2,1,0:T(8,128)(2,1)S(1)}, u32[]{:S(2)}, u32[]{:S(2)}) collective-permute-start(bf16[4,24,32,128]{3,2,1,0:T(8,128)(2,1)S(1)} %get-tuple-element.34), channel_id=1, source_target_pairs={{0,192},{64,0},{128,64},{192,128},{16,208},{80,16},{144,80},{208,1... | collective-permute-start | bytes 2359304 | tf_op jit(solution)/shard_map/ppermute | solution.py:460
  97.5 6.4 %collective-permute-start.10 = (bf16[24,32,128]{2,1,0:T(8,128)(2,1)S(1)}, bf16[24,32,128]{2,1,0:T(8,128)(2,1)S(1)}, u32[]{:S(2)}, u32[]{:S(2)}) collective-permute-start(bf16[24,32,128]{2,1,0:T(8,128)(2,1)S(1)} %get-tuple-element.47), channel_id=1, source_target_pairs={{0,32},{16,48},{32,0},{48,16},{64,96},{80,112},{96,64},{112,80},{1... | collective-permute-start | bytes 589832 | tf_op jit(solution)/shard_map/ppermute | solution.py:460
  100.0 5.7 %collective-permute-start.11 = (bf16[24,32,128]{2,1,0:T(8,128)(2,1)S(1)}, bf16[24,32,128]{2,1,0:T(8,128)(2,1)S(1)}, u32[]{:S(2)}, u32[]{:S(2)}) collective-permute-start(bf16[24,32,128]{2,1,0:T(8,128)(2,1)S(1)} %get-tuple-element.46), channel_id=1, source_target_pairs={{0,48},{16,0},{32,16},{48,32},{64,112},{80,64},{96,80},{112,96},{1... | collective-permute-start | bytes 589832 | tf_op jit(solution)/shard_map/ppermute | solution.py:460
  100.9 5.7 %collective-permute-start.9 = (bf16[24,32,128]{2,1,0:T(8,128)(2,1)S(1)}, bf16[24,32,128]{2,1,0:T(8,128)(2,1)S(1)}, u32[]{:S(2)}, u32[]{:S(2)}) collective-permute-start(bf16[24,32,128]{2,1,0:T(8,128)(2,1)S(1)} %get-tuple-element.45), channel_id=1, source_target_pairs={{0,16},{16,32},{32,48},{48,0},{64,80},{80,96},{96,112},{112,64},{1... | collective-permute-start | bytes 589832 | tf_op jit(solution)/shard_map/ppermute | solution.py:460
  107.4 17.2 %all-to-all-start.1 = ((bf16[16,32,128]{2,1,0:T(8,128)(2,1)}), bf16[16,32,128]{2,1,0:T(8,128)(2,1)S(1)}, u32[]{:S(2)}, u32[]{:S(2)}) async-start(bf16[16,32,128]{2,1,0:T(8,128)(2,1)} %fusion.3), calls=%async_computation.2 | async-start | bytes 262144 | tf_op jit(solution)/shard_map/all_to_all | solution.py:575
  124.7 6.2 %collective-permute-start.12 = (bf16[24,32,128]{2,1,0:T(8,128)(2,1)S(1)}, bf16[24,32,128]{2,1,0:T(8,128)(2,1)S(1)}, u32[]{:S(2)}, u32[]{:S(2)}) collective-permute-start(bf16[24,32,128]{2,1,0:T(8,128)(2,1)S(1)} %get-tuple-element.49), channel_id=1, source_target_pairs={{0,16},{16,32},{32,48},{48,0},{64,80},{80,96},{96,112},{112,64},{1... | collective-permute-start | bytes 589832 | tf_op jit(solution)/shard_map/ppermute | solution.py:460
  126.4 6.9 %collective-permute-start.13 = (bf16[24,32,128]{2,1,0:T(8,128)(2,1)S(1)}, bf16[24,32,128]{2,1,0:T(8,128)(2,1)S(1)}, u32[]{:S(2)}, u32[]{:S(2)}) collective-permute-start(bf16[24,32,128]{2,1,0:T(8,128)(2,1)S(1)} %get-tuple-element.49), channel_id=1, source_target_pairs={{0,32},{16,48},{32,0},{48,16},{64,96},{80,112},{96,64},{112,80},{1... | collective-permute-start | bytes 589832 | tf_op jit(solution)/shard_map/ppermute | solution.py:460
  128.2 5.3 %collective-permute-start.14 = (bf16[24,32,128]{2,1,0:T(8,128)(2,1)S(1)}, bf16[24,32,128]{2,1,0:T(8,128)(2,1)S(1)}, u32[]{:S(2)}, u32[]{:S(2)}) collective-permute-start(bf16[24,32,128]{2,1,0:T(8,128)(2,1)S(1)} %get-tuple-element.49), channel_id=1, source_target_pairs={{0,48},{16,0},{32,16},{48,32},{64,112},{80,64},{96,80},{112,96},{1... | collective-permute-start | bytes 589832 | tf_op jit(solution)/shard_map/ppermute | solution.py:460
  133.6 20.8 %collective-permute-start.15 = (bf16[4,24,32,128]{3,2,1,0:T(8,128)(2,1)S(1)}, bf16[4,24,32,128]{3,2,1,0:T(8,128)(2,1)S(1)}, u32[]{:S(2)}, u32[]{:S(2)}) collective-permute-start(bf16[4,24,32,128]{3,2,1,0:T(8,128)(2,1)S(1)} %pad_maximum_fusion.full_0), channel_id=1, source_target_pairs={{0,64},{64,128},{128,192},{192,0},{16,80},{80,144},{144,208},{208,... | collective-permute-start | bytes 2359304 | tf_op jit(solution)/shard_map/ppermute | solution.py:460
  133.7 20.8 %collective-permute-start.16 = (bf16[4,24,32,128]{3,2,1,0:T(8,128)(2,1)S(1)}, bf16[4,24,32,128]{3,2,1,0:T(8,128)(2,1)S(1)}, u32[]{:S(2)}, u32[]{:S(2)}) collective-permute-start(bf16[4,24,32,128]{3,2,1,0:T(8,128)(2,1)S(1)} %pad_maximum_fusion.full_0), channel_id=1, source_target_pairs={{0,128},{64,192},{128,0},{192,64},{16,144},{80,208},{144,16},{208,... | collective-permute-start | bytes 2359304 | tf_op jit(solution)/shard_map/ppermute | solution.py:460
  135.9 19.2 %collective-permute-start.17 = (bf16[4,24,32,128]{3,2,1,0:T(8,128)(2,1)S(1)}, bf16[4,24,32,128]{3,2,1,0:T(8,128)(2,1)S(1)}, u32[]{:S(2)}, u32[]{:S(2)}) collective-permute-start(bf16[4,24,32,128]{3,2,1,0:T(8,128)(2,1)S(1)} %pad_maximum_fusion.full_0), channel_id=1, source_target_pairs={{0,192},{64,0},{128,64},{192,128},{16,208},{80,16},{144,80},{208,1... | collective-permute-start | bytes 2359304 | tf_op jit(solution)/shard_map/ppermute | solution.py:460
Sparse Core Ops, SparseCore 0:
  10.8 51.5 all-gather.2
  97.5 61.9 reduce-scatter.1
